TPU v7x, 32 devices: a whole 2x2x4 slice. The times are simulated.
32 devices in a mesh: row: 4 (over x, core), col: 8 (over z, y).
Axes of the slice: x: 2, y: 2, z: 4, core: 2. Of those that a mesh axis runs over, the one named last changes fastest.
Arguments:
- object_field: float32 [2, 2048, 4096], P(None, 'row', 'col'), may hold values from -5 to 5
- probe: float32 [2, 2, 256, 256], replicated, may hold values from -5 to 5
- amplitudes: float32 [256, 256, 256], P(('row', 'col')), may hold values from 0 to 2.5
- positions: int32 [256, 2], P(('row', 'col')), may hold values from 0 to 3840, as said below
- counts: int32 [32], P(('row', 'col')), may hold values from 1 to 8, as said below
Outputs:
- new_object: float32 [2, 2048, 4096], P(None, 'row', 'col')
- new_probe: float32 [2, 2, 256, 256], replicated
Inputs may be any that keep to these rules, and one draw needn't show every extreme that they name: `positions`: each slot's patch lies inside the object, and its top-left pixel lies in the tile of the device that holds the slot. `counts`: one device holds exactly 8 live slots in every draw; the others fewer.
All inputs are finite; a program needn't handle non-finite values.
Results may differ from a plain program's by a relative error of at most 0.0003.
Values sent between devices are 32-bit elements; how exact they have to be, the bound alone decides.
No kernel may reach another device: no remote copies, remote signals or barrier semaphores. Data moves between devices by JAX's collectives and lax.ppermute only.
A program may use at most 256 MiB of HBM per device.

v0:
```python
import functools
import math

import jax
import jax.numpy as jnp
import ml_dtypes
import numpy as np
from jax import lax
from jax.experimental import pallas as pl
from jax.experimental.pallas import tpu as pltpu
from jax.sharding import PartitionSpec as P

F32 = jnp.float32
BF16 = jnp.bfloat16
MIB = 1024 * 1024
LONG = pl.CostEstimate(flops=30_000_000_000, bytes_accessed=4_000_000, transcendentals=0)
SHORT = pl.CostEstimate(flops=0, bytes_accessed=1_000_000, transcendentals=0)
FLOOR = 0.3


def split_np(table):
    high = table.astype(ml_dtypes.bfloat16)
    low = (table - high.astype(np.float64)).astype(ml_dtypes.bfloat16)
    return high, low


def dft_tables(length):
    half = length // 2
    q = np.arange(half)[:, None]
    n = np.arange(half)[None, :]
    forward = []
    for odd in range(2):
        phase = (n * (2 * q + odd)) % length
        angle = phase * (-2.0 * math.pi / length)
        re = np.cos(angle) / math.sqrt(length)
        im = np.sin(angle) / math.sqrt(length)
        forward.append(np.stack(split_np(np.block([[re, -im], [im, re]]))))
    forward = np.stack(forward)
    return forward, np.ascontiguousarray(forward.transpose(0, 1, 3, 2))


def in_hbm(array):
    return pltpu.with_memory_space_constraint(array, pltpu.HBM)


def dot(a, b):
    return jnp.dot(a, b, preferred_element_type=F32)


def split(x):
    high = x.astype(BF16)
    return high, (x - high.astype(F32)).astype(BF16)


def roll_rows(x, shift):
    return pltpu.roll(x.reshape(x.shape[0] // 8, 8, x.shape[1]), shift, 1)


def roll_rows(x, shift):
    return pltpu.roll(x.reshape(x.shape[0] // 8, 8, x.shape[1]), shift, 1)


def roll_rows(x, shift):
    return pltpu.roll(x.reshape(x.shape[0] // 8, 8, x.shape[1]), shift, 1)


def roll_rows(x, shift):
    return pltpu.roll(x.reshape(x.shape[0] // 8, 8, x.shape[1]), shift, 1)


def split_three(x):
    high = x.astype(BF16)
    rest = x - high.astype(F32)
    middle = rest.astype(BF16)
    return high, middle, (rest - middle.astype(F32)).astype(BF16)


def add_shifted(template, grid, where_t, where_g, top, left, size):
    top_s = top & 7
    top_b = pl.multiple_of(top - top_s, 8)
    left_s = left & 127
    left_b = pl.multiple_of(left - left_s, 128)
    step = 24
    wrapped = lax.broadcasted_iota(jnp.int32, (step, 128), 1) < left_s
    wrapped_rows = lax.broadcasted_iota(jnp.int32, (step // 8, 8, 128), 1) < top_s
    zero = jnp.zeros((step, 128), F32)
    blocks = size // 128
    for at in range(0, size + 8, step):
        parts = []
        for j in range(blocks):
            x = roll_rows(template[where_t + (pl.ds(at, step + 8), pl.ds(128 * j, 128))], top_s)
            x = jnp.where(wrapped_rows, x[:-1], x[1:]).reshape(step, 128)
            parts.append(pltpu.roll(x, left_s, 1))
        for j in range(blocks + 1):
            before = parts[j - 1] if j > 0 else zero
            after = parts[j] if j < blocks else zero
            spot = where_g + (pl.ds(top_b + at, step), pl.ds(left_b + 128 * j, 128))
            grid[spot] += jnp.where(wrapped, before, after)


def take_shifted(field, where, top, left, at, step, size):
    top_s = top & 7
    top_b = pl.multiple_of(top - top_s, 8)
    left_s = left & 127
    left_b = pl.multiple_of(left - left_s, 128)
    back = (128 - left_s) & 127
    keep = lax.broadcasted_iota(jnp.int32, (step + 8, 128), 1) < 128 - left_s
    keep_rows = lax.broadcasted_iota(jnp.int32, (step // 8, 8, 128), 1) < 8 - top_s
    blocks = size // 128
    parts = [
        pltpu.roll(field[where + (pl.ds(top_b + at, step + 8), pl.ds(left_b + 128 * j, 128))], back, 1)
        for j in range(blocks + 1)
    ]
    pieces = []
    for j in range(blocks):
        x = roll_rows(jnp.where(keep, parts[j], parts[j + 1]), (8 - top_s) & 7)
        pieces.append(jnp.where(keep_rows, x[:-1], x[1:]).reshape(step, 128))
    return jnp.concatenate(pieces, axis=1)


def light_kernel(slots, origin, meta, probe_h, bottom, corner, lower, inverse_light, probe, template, grid, notes, sems):
    size = probe.shape[2]
    tile_rows, tile_cols = inverse_light.shape
    copies = [
        pltpu.make_async_copy(spill.at[0, pl.ds(spill.shape[1] - 8, 8), pl.ds(0, 128)], notes.at[i], sems.at[i])
        for i, spill in enumerate((bottom, corner, lower))
    ]
    copy = pltpu.make_async_copy(probe_h, probe, sems.at[3])
    copy.start()
    for item in copies:
        item.start()
    template[0:8, :] = jnp.zeros((8, size), F32)
    template[8 + size :, :] = jnp.zeros((8, size), F32)
    copy.wait()
    for at in range(0, size, 32):
        rows = pl.ds(at, 32)
        total = jnp.zeros((32, size), F32)
        for m in range(probe.shape[0]):
            total += probe[m, 0, rows] * probe[m, 0, rows] + probe[m, 1, rows] * probe[m, 1, rows]
        template[pl.ds(8 + at, 32), :] = total

    @pl.loop(0, tile_rows // 32)
    def _(step):
        rows = pl.ds(pl.multiple_of(size + step * 32, 32), 32)
        grid[rows, size : size + tile_cols] = jnp.zeros((32, tile_cols), F32)

    def add(top, left):
        @pl.when((top > 0) & (left > 0))
        def _():
            add_shifted(template, grid, (), (), top, left, size)

    @pl.loop(0, meta[0, 2 * slots])
    def _(slot):
        add(meta[0, 2 * slot] + size, meta[0, 2 * slot + 1] + size)

    for item in copies:
        item.wait()
    for device in range(3):

        @pl.loop(0, notes[device, 0, 2 * slots].astype(jnp.int32))
        def _(slot):
            top = notes[device, 0, 2 * slot].astype(jnp.int32) - meta[0, origin]
            left = notes[device, 0, 2 * slot + 1].astype(jnp.int32) - meta[0, origin + 1]
            add(top + size, left + size)

    @pl.loop(0, tile_rows // 32)
    def _(step):
        rows = pl.ds(pl.multiple_of(size + step * 32, 32), 32)
        out_rows = pl.ds(pl.multiple_of(step * 32, 32), 32)
        inverse_light[out_rows, :] = 1.0 / (grid[rows, size : size + tile_cols] + 1.0)


def light(meta, slots, origin, probe, bottom, corner, lower, tile_shape):
    size = probe.shape[2]
    hbm = pl.BlockSpec(memory_space=pltpu.HBM)
    anywhere = pl.BlockSpec(memory_space=pl.ANY)
    return pl.pallas_call(
        functools.partial(light_kernel, slots, origin),
        out_shape=jax.ShapeDtypeStruct(tile_shape, F32),
        in_specs=[pl.BlockSpec(memory_space=pltpu.SMEM), hbm] + [anywhere] * 3,
        out_specs=pl.BlockSpec(memory_space=pltpu.VMEM),
        scratch_shapes=[
            pltpu.VMEM(probe.shape, F32),
            pltpu.VMEM((size + 16, size), F32),
            pltpu.VMEM((tile_shape[0] + 2 * size, tile_shape[1] + 2 * size), F32),
            pltpu.SMEM((3, 8, 128), F32),
            pltpu.SemaphoreType.DMA((4,)),
        ],
        compiler_params=pltpu.CompilerParams(vmem_limit_bytes=8 * MIB),
        cost_estimate=pl.CostEstimate(flops=4_000_000_000, bytes_accessed=1_000_000, transcendentals=0),
        name="light",
    )(meta, in_hbm(probe), bottom, corner, lower)


def arrange_kernel(meta, amplitudes, out, given, moved, in_sems, out_sems):
    slots, size, _ = amplitudes.shape
    count = meta[0, 2 * slots]

    def load(slot):
        return pltpu.make_async_copy(amplitudes.at[slot], given.at[slot], in_sems.at[slot])

    def store(slot):
        return pltpu.make_async_copy(moved.at[slot], out.at[slot], out_sems.at[slot])

    @pl.loop(0, count)
    def _(slot):
        load(slot).start()

    first = lax.broadcasted_iota(jnp.int32, (size, size), 0)
    second = lax.broadcasted_iota(jnp.int32, (size, size), 1)
    half = size // 2

    def source(index):
        return jnp.where(index < half, 2 * index, 2 * index - (size - 1))

    rows = (source(first) == second).astype(F32).astype(BF16)
    cols = (source(second) == first).astype(F32).astype(BF16)
    rows = jnp.concatenate([rows, rows], axis=1)
    cols = jnp.concatenate([cols, cols], axis=0)

    def each(pair, act):
        act(2 * pair)

        @pl.when(2 * pair + 1 < count)
        def _():
            act(2 * pair + 1)

    @pl.loop(0, (count + 1) // 2)
    def _(pair):
        each(pair, lambda slot: load(slot).wait())
        x = [dot(rows, jnp.concatenate(split(given[2 * pair + k]), axis=0)) for k in range(2)]
        for k in range(2):
            moved[2 * pair + k] = dot(jnp.concatenate(split(x[k]), axis=1), cols)
        each(pair, lambda slot: store(slot).start())

    @pl.loop(0, count)
    def _(slot):
        store(slot).wait()


def arrange(meta, amplitudes):
    slots = amplitudes.shape[0]
    hbm = pl.BlockSpec(memory_space=pltpu.HBM)
    return pl.pallas_call(
        arrange_kernel,
        out_shape=pltpu.HBM(amplitudes.shape, F32),
        in_specs=[pl.BlockSpec(memory_space=pltpu.SMEM), hbm],
        out_specs=hbm,
        scratch_shapes=[
            pltpu.VMEM(amplitudes.shape, F32),
            pltpu.VMEM(amplitudes.shape, F32),
            pltpu.SemaphoreType.DMA((slots,)),
            pltpu.SemaphoreType.DMA((slots,)),
        ],
        compiler_params=pltpu.CompilerParams(vmem_limit_bytes=8 * MIB),
        cost_estimate=LONG,
        name="arrange",
    )(meta, in_hbm(amplitudes))


def three_left(table, t):
    return jnp.concatenate([table[t, 0], table[t, 0], table[t, 1]], axis=1)


def three_right(table, v):
    return jnp.concatenate([table[v, 0], table[v, 0], table[v, 1]], axis=0)


def weave(first, second):
    total = max(len(first), len(second))
    done = [0, 0]
    for i in range(1, total + 1):
        for k, pieces in enumerate((first, second)):
            while done[k] * total < i * len(pieces):
                pieces[done[k]]()
                done[k] += 1


def slots_kernel(
    needs_rim, meta, probe, amplitudes, sources, tables, note, state, outs,
    amp, forward_t, backward_t, chosen, patch_f, patch_b, x_f, y_f, z_f, g_s, x_b, z_b, back, template,
    load_sems, amp_sems, out_sems,
):
    ext, grid, probe_out = state
    size = probe.shape[2]
    half = size // 2
    modes = probe.shape[0]
    slots = amplitudes.shape[0]
    tile_rows, tile_cols = (n - size for n in ext.shape[1:])
    step = 32
    fine = 16

    body_rows, rim_rows = pl.ds(0, tile_rows), pl.ds(tile_rows, size)
    body_cols, rim_cols = pl.ds(0, tile_cols), pl.ds(tile_cols, size)
    if needs_rim:
        places = [
            ext.at[:, pl.ds(0, size), rim_cols],
            ext.at[:, pl.ds(size, tile_rows - size), rim_cols],
            ext.at[:, rim_rows, rim_cols],
        ]
    else:
        places = [ext.at[:, body_rows, body_cols], ext.at[:, rim_rows, body_cols]]
    places += [forward_t, backward_t]
    loads = [
        pltpu.make_async_copy(source, place, load_sems.at[i])
        for i, (source, place) in enumerate(zip([*sources, *tables], places))
    ]
    for load in loads:
        load.start()

    def amp_copy(slot):
        return pltpu.make_async_copy(amplitudes.at[slot], amp.at[slot], amp_sems.at[slot])

    def choose(slot, found):
        beyond = meta[0, 2 * slot + 1] + size > tile_cols
        wanted = beyond if needs_rim else jnp.logical_not(beyond)

        @pl.when(wanted)
        def _():
            chosen[found] = slot
            amp_copy(slot).start()

        return found + wanted.astype(jnp.int32)

    count = lax.fori_loop(0, meta[0, 2 * slots], choose, jnp.zeros((), jnp.int32))

    if not needs_rim:

        @pl.loop(0, (tile_rows + size) // step)
        def _(at):
            rows = pl.ds(pl.multiple_of(at * step, step), step)
            for c in range(2):
                grid[c, rows, :] = jnp.zeros((step, tile_cols + size), F32)

        @pl.loop(0, size // step)
        def _(at):
            rows = pl.ds(pl.multiple_of(at * step, step), step)
            for c in range(2 * modes + 1):
                probe_out[c, rows, :] = jnp.zeros((step, size), F32)

    for c in range(2):
        template[c, 0:8, :] = jnp.zeros((8, size), F32)
        template[c, 8 + size :, :] = jnp.zeros((8, size), F32)
    for load in loads:
        load.wait()

    def corner(slot):
        return meta[0, 2 * slot], meta[0, 2 * slot + 1]

    def forward(slot):
        top, left = corner(slot)

        def take(at):
            for c in range(2):
                patch_f[c, pl.ds(at, step), :] = take_shifted(ext, (c,), top, left, at, step, size)

        def fold_rows(m, at):
            cols = pl.ds(m * size, size)
            parts = []
            for base in (at, half + at):
                rows = pl.ds(base, fine)
                pr, pi = patch_f[0, rows, :], patch_f[1, rows, :]
                qr, qi = probe[m, 0, rows, :], probe[m, 1, rows, :]
                parts.append((qr * pr - qi * pi, qr * pi + qi * pr))
            for c in range(2):
                rows = pl.ds(c * half + at, fine)
                for t, value in enumerate((parts[0][c] + parts[1][c], parts[0][c] - parts[1][c])):
                    x_f[t, 0, rows, cols], x_f[t, 1, rows, cols] = split(value)

        def dft_rows(m, t):
            cols = pl.ds(m * size, size)
            high = x_f[t, 0, :, cols]
            u = dot(three_left(forward_t, t), jnp.concatenate([high, x_f[t, 1, :, cols], high], axis=0))
            rows = pl.ds(m * size + t * half, half)
            for v, value in enumerate((u[:, :half] + u[:, half:], u[:, :half] - u[:, half:])):
                high, low = split(value)
                for c in range(2):
                    lanes = pl.ds(c * half, half)
                    y_f[v, 0, rows, lanes] = high[c * half : (c + 1) * half]
                    y_f[v, 1, rows, lanes] = low[c * half : (c + 1) * half]

        def dft_cols(v):
            high = y_f[v, 0]
            z_f[v] = dot(jnp.concatenate([high, y_f[v, 1], high], axis=1), three_right(backward_t, v))

        def scale(v, at):
            if v == 0 and at == 0:
                amp_copy(slot).wait()
            waves = [z_f[v, pl.ds(m * size + at, fine), :] for m in range(modes)]
            total = jnp.zeros((fine, half), F32)
            for wave in waves:
                total += wave[:, :half] * wave[:, :half] + wave[:, half:] * wave[:, half:]
            measured = amp[slot, pl.ds(at, fine), pl.ds(v * half, half)]
            factor = measured * lax.rsqrt(jnp.maximum(total, FLOOR * FLOOR)) - 1.0
            factor = jnp.concatenate([factor, factor], axis=1)
            for m in range(modes):
                rows = pl.ds(m * size + at, fine)
                g_s[v, 0, rows, :], g_s[v, 1, rows, :] = split(waves[m] * factor)

        pieces = [(take, at) for at in range(0, size, step)]
        for m in range(modes):
            pieces += [(fold_rows, m, at) for at in range(0, half, fine)]
            pieces += [(dft_rows, m, t) for t in range(2)]
        pieces += [(dft_cols, v) for v in range(2)]
        pieces += [(scale, v, at) for v in range(2) for at in range(0, size, fine)]
        return [functools.partial(*piece) for piece in pieces]

    def backward(slot):
        top, left = corner(slot)

        def dft_cols(v):
            high = g_s[v, 0]
            z_b[v] = dot(jnp.concatenate([high, g_s[v, 1], high], axis=1), three_right(forward_t, v))

        def unfold_cols(m, t, at):
            rows = pl.ds(m * size + t * half + at, step)
            even, odd = z_b[0, rows, :], z_b[1, rows, :]
            for v, value in enumerate((even + odd, even - odd)):
                high, low = split(value)
                cols = pl.ds(m * size + v * half, half)
                for c in range(2):
                    spot = pl.ds(c * half + at, step)
                    x_b[t, 0, spot, cols] = high[:, c * half : (c + 1) * half]
                    x_b[t, 1, spot, cols] = low[:, c * half : (c + 1) * half]

        def dft_rows(m, t):
            cols = pl.ds(m * size, size)
            high = x_b[t, 0, :, cols]
            back[m, t] = dot(three_left(backward_t, t), jnp.concatenate([high, x_b[t, 1, :, cols], high], axis=0))

        def gradients(at):
            waves = []
            for m in range(modes):
                pair = []
                for c in range(2):
                    rows = pl.ds(c * half + at, fine)
                    even, odd = back[m, 0, rows, :], back[m, 1, rows, :]
                    pair.append((even + odd, even - odd))
                waves.append(pair)
            for h in range(2):
                rows = pl.ds(h * half + at, fine)
                pr, pi = patch_b[0, rows, :], patch_b[1, rows, :]
                grad_r = jnp.zeros((fine, size), F32)
                grad_i = jnp.zeros((fine, size), F32)
                for m in range(modes):
                    br, bi = waves[m][0][h], waves[m][1][h]
                    qr, qi = probe[m, 0, rows, :], probe[m, 1, rows, :]
                    grad_r += qr * br + qi * bi
                    grad_i += qr * bi - qi * br
                    probe_out[2 * m, rows, :] += pr * br + pi * bi
                    probe_out[2 * m + 1, rows, :] += pr * bi - pi * br
                probe_out[2 * modes, rows, :] += pr * pr + pi * pi
                spot = pl.ds(8 + h * half + at, fine)
                template[0, spot, :] = grad_r
                template[1, spot, :] = grad_i

        def add(c):
            add_shifted(template, grid, (c,), (c,), top, left, size)

        pieces = [(dft_cols, v) for v in range(2)]
        for m in range(modes):
            pieces += [(unfold_cols, m, t, at) for t in range(2) for at in range(0, half, step)]
            pieces += [(dft_rows, m, t) for t in range(2)]
        pieces += [(gradients, at) for at in range(0, half, fine)]
        pieces += [(add, c) for c in range(2)]
        return [functools.partial(*piece) for piece in pieces]

    def hand_over():
        for at in range(0, size, step):
            for c in range(2):
                patch_b[c, pl.ds(at, step), :] = patch_f[c, pl.ds(at, step), :]

    @pl.when(count > 0)
    def _():
        weave(forward(chosen[0]), [])
        hand_over()

        def visit(index, _):
            weave(backward(chosen[index]), forward(chosen[index + 1]))
            hand_over()
            return 0

        lax.fori_loop(0, count - 1, visit, 0)
        weave(backward(chosen[count - 1]), [])

    if needs_rim:
        top, bottom = pl.ds(0, size), pl.ds(size, tile_rows - size)
        parts = [
            (grid.at[:, body_rows, body_cols], outs[0]),
            (grid.at[:, bottom, rim_cols], outs[1].at[:, pl.ds(0, tile_rows - size)]),
            (note, outs[1].at[0, pl.ds(tile_rows - size, 8)]),
            (grid.at[:, top, rim_cols], outs[2]),
            (grid.at[:, rim_rows, rim_cols], outs[3].at[:, top]),
            (note, outs[3].at[0, pl.ds(size, 8)]),
            (grid.at[:, rim_rows, body_cols], outs[4].at[:, top]),
            (probe_out.at[:, pl.ds(pl.multiple_of(meta[0, 2 * slots + 1] * half, half), half)], outs[5]),
        ]
        stores = [pltpu.make_async_copy(part, out, out_sems.at[i]) for i, (part, out) in enumerate(parts)]
        for store in stores:
            store.start()
        for store in stores:
            store.wait()


def scratch_for(size, modes, slots):
    return [
        pltpu.VMEM((slots, size, size), F32),
        pltpu.VMEM((2, 2, size, size), BF16),
        pltpu.VMEM((2, 2, size, size), BF16),
        pltpu.SMEM((slots,), jnp.int32),
        pltpu.VMEM((2, size, size), F32),
        pltpu.VMEM((2, size, size), F32),
        pltpu.VMEM((2, 2, size, modes * size), BF16),
        pltpu.VMEM((2, 2, modes * size, size), BF16),
        pltpu.VMEM((2, modes * size, size), F32),
        pltpu.VMEM((2, 2, modes * size, size), BF16),
        pltpu.VMEM((2, 2, size, modes * size), BF16),
        pltpu.VMEM((2, modes * size, size), F32),
        pltpu.VMEM((modes, 2, size, size), F32),
        pltpu.VMEM((2, size + 16, size), F32),
        pltpu.SemaphoreType.DMA((5,)),
        pltpu.SemaphoreType.DMA((slots,)),
        pltpu.SemaphoreType.DMA((8,)),
    ]


SLOTS_COST = pl.CostEstimate(flops=12_000_000_000, bytes_accessed=16_000_000, transcendentals=0)


def visit_inside(meta, probe, amplitudes, tile, lower):
    size, modes, slots = probe.shape[2], probe.shape[0], amplitudes.shape[0]
    rows, cols = tile.shape[1:]
    tables = [jnp.asarray(item) for item in dft_tables(size)]
    vmem = pl.BlockSpec(memory_space=pltpu.VMEM)
    hbm = pl.BlockSpec(memory_space=pltpu.HBM)
    field = pltpu.VMEM((2, rows + size, cols + size), F32)

    def kernel(meta, probe, amplitudes, tile, lower, forward_h, backward_h, *refs):
        state, scratch = refs[:3], refs[3:]
        slots_kernel(
            False, meta, probe, amplitudes, [tile, lower], [forward_h, backward_h], None, state, None, *scratch
        )

    return pl.pallas_call(
        kernel,
        out_shape=[field, field, pltpu.VMEM((2 * modes + 1, size, size), F32)],
        in_specs=[pl.BlockSpec(memory_space=pltpu.SMEM), vmem, hbm, hbm, pl.BlockSpec(memory_space=pl.ANY), hbm, hbm],
        out_specs=[vmem] * 3,
        scratch_shapes=scratch_for(size, modes, slots),
        compiler_params=pltpu.CompilerParams(vmem_limit_bytes=28 * MIB),
        cost_estimate=SLOTS_COST,
        name="slots_inside",
    )(meta, probe, in_hbm(amplitudes), in_hbm(tile), lower, *map(in_hbm, tables))


def visit_beyond(meta, probe, amplitudes, rims, note, state):
    size, modes, slots = probe.shape[2], probe.shape[0], amplitudes.shape[0]
    rows, cols = (n - size for n in state[0].shape[1:])
    tables = [jnp.asarray(item) for item in dft_tables(size)]
    vmem = pl.BlockSpec(memory_space=pltpu.VMEM)
    hbm = pl.BlockSpec(memory_space=pltpu.HBM)
    anywhere = pl.BlockSpec(memory_space=pl.ANY)
    shapes = [
        (2, rows - size + 8, size),
        (2, size, size),
        (2, size + 8, size),
        (2, size + 8, cols),
        (2 * modes + 1, size // 2, size),
    ]

    def kernel(meta, probe, amplitudes, forward_h, backward_h, *refs):
        rims, note, refs = refs[:3], refs[3], refs[7:]
        state, outs, scratch = refs[:3], refs[3:9], refs[9:]
        slots_kernel(True, meta, probe, amplitudes, rims, [forward_h, backward_h], note, state, outs, *scratch)

    out = pl.pallas_call(
        kernel,
        out_shape=[pltpu.VMEM(item.shape, item.dtype) for item in state]
        + [pltpu.HBM((2, rows, cols), F32)]
        + [jax.ShapeDtypeStruct(shape, F32) for shape in shapes],
        in_specs=[pl.BlockSpec(memory_space=pltpu.SMEM), vmem] + [hbm] * 3 + [anywhere] * 4 + [vmem] * 3,
        out_specs=[vmem] * 3 + [hbm] + [anywhere] * 5,
        input_output_aliases={9 + i: i for i in range(3)},
        scratch_shapes=scratch_for(size, modes, slots),
        compiler_params=pltpu.CompilerParams(vmem_limit_bytes=28 * MIB),
        cost_estimate=SLOTS_COST,
        name="slots_beyond",
    )(meta, probe, *map(in_hbm, [amplitudes, *tables]), *rims, note, *state)
    return (*out[3:], out[2])


def finish_kernel(
    chosen, own, top, bottom, lower, scale, tile, out, own_s, right_s, lower_s, scale_s, tile_s, in_sems, out_sems
):
    size = right_s.shape[2]
    block = 128
    blocks = own_s.shape[1] // block

    def copies(i):
        rows = pl.ds(i * block, block)
        pairs = [
            (own.at[:, rows], own_s.at[:, rows]),
            (scale.at[rows], scale_s.at[rows]),
            (tile.at[:, rows], tile_s.at[:, rows]),
        ]
        if i < size // block:
            pairs.append((top.at[:, rows], right_s.at[:, rows]))
            pairs.append((lower.at[:, rows], lower_s.at[:, rows]))
        else:
            pairs.append((bottom.at[:, pl.ds(i * block - size, block)], right_s.at[:, rows]))
        return [pltpu.make_async_copy(a, b, in_sems.at[i, k]) for k, (a, b) in enumerate(pairs)]

    loads = {i: copies(i) for i in range(blocks) if chosen(i * block)}
    for load in loads.values():
        for copy in load:
            copy.start()
    stores = []
    for i in loads:
        for copy in loads[i]:
            copy.wait()
        rows = pl.ds(i * block, block)
        for at in range(i * block, (i + 1) * block, 32):
            part = pl.ds(at, 32)
            for c in range(2):
                near, far = own_s[c, part, :size] + right_s[c, part, :], own_s[c, part, size:]
                if i < size // block:
                    near, far = near + lower_s[c, part, :size], far + lower_s[c, part, size:]
                own_s[c, part, :size] = tile_s[c, part, :size] + near * scale_s[part, :size]
                own_s[c, part, size:] = tile_s[c, part, size:] + far * scale_s[part, size:]
        stores.append(pltpu.make_async_copy(own_s.at[:, rows], out.at[:, rows], out_sems.at[i]))
        stores[-1].start()
    for store in stores:
        store.wait()


def finish(own, top, bottom, lower, inverse_light, tile, before=None):
    rows, cols = tile.shape[1:]
    size = bottom.shape[2]
    anywhere = pl.BlockSpec(memory_space=pl.ANY)
    hbm = pl.BlockSpec(memory_space=pltpu.HBM)
    if before is None:

        def kernel(own, bottom, scale, tile, *refs):
            finish_kernel(lambda at: at >= size, own, None, bottom, None, scale, tile, *refs)

        operands = (in_hbm(own), bottom, inverse_light, in_hbm(tile))
        in_specs = [hbm, anywhere, anywhere, hbm]
        aliases = {}
    else:

        def kernel(before, own, top, lower, scale, tile, *refs):
            finish_kernel(lambda at: at < size, own, top, None, lower, scale, tile, *refs)

        operands = (in_hbm(before), in_hbm(own), top, lower, inverse_light, in_hbm(tile))
        in_specs = [hbm, hbm, anywhere, anywhere, anywhere, hbm]
        aliases = {0: 0}
    return pl.pallas_call(
        kernel,
        out_shape=pltpu.HBM(tile.shape, F32),
        in_specs=in_specs,
        out_specs=hbm,
        input_output_aliases=aliases,
        scratch_shapes=[
            pltpu.VMEM(tile.shape, F32),
            pltpu.VMEM((2, rows, size), F32),
            pltpu.VMEM((2, size, cols), F32),
            pltpu.VMEM((rows, cols), F32),
            pltpu.VMEM(tile.shape, F32),
            pltpu.SemaphoreType.DMA((rows // 128, 5)),
            pltpu.SemaphoreType.DMA((rows // 128,)),
        ],
        compiler_params=pltpu.CompilerParams(vmem_limit_bytes=12 * MIB),
        cost_estimate=pl.CostEstimate(flops=2_000_000_000, bytes_accessed=6_000_000, transcendentals=0),
        name="finish_far" if before is None else "finish_near",
    )(*operands)


def from_behind(array, axis, by):
    count = lax.axis_size(axis)
    pairs = [(i, i + by) for i in range(count) if 0 <= i + by < count]
    return lax.ppermute(array, axis, pairs)


def exchange(array, axis, bit):
    count = lax.axis_size(axis)
    return lax.ppermute(array, axis, [(i, i ^ bit) for i in range(count)])


def together(*arrays):
    return lax.optimization_barrier(arrays)


def cut(tile, regions, cost, name):
    def kernel(tile, *refs):
        sems = refs[-1]
        copies = [
            pltpu.make_async_copy(tile.at[:, pl.ds(at, height), pl.ds(0, width)], out, sems.at[i])
            for i, ((at, height, width), out) in enumerate(zip(regions, refs[:-1]))
        ]
        for copy in copies:
            copy.start()
        for copy in copies:
            copy.wait()

    return pl.pallas_call(
        kernel,
        out_shape=[jax.ShapeDtypeStruct((2, height, width), F32) for _, height, width in regions],
        in_specs=[pl.BlockSpec(memory_space=pltpu.HBM)],
        out_specs=[pl.BlockSpec(memory_space=pltpu.VMEM)] * len(regions),
        scratch_shapes=[pltpu.SemaphoreType.DMA((len(regions),))],
        compiler_params=pltpu.CompilerParams(vmem_limit_bytes=4 * MIB),
        cost_estimate=cost,
        name=name,
    )(in_hbm(tile))


def fold(places, index, mine, got, upper):
    count, half, width = got.shape
    quarter = half // 2

    def kernel(places, mine, got, send, keep):
        base = 0 if index is None else places[0, index] * half
        for k, out in ((1 - places[0, upper], send), (places[0, upper], keep)):
            for c in range(count):
                out[c] = (
                    mine[c, pl.ds(pl.multiple_of(base + k * quarter, quarter), quarter), :]
                    + got[c, pl.ds(pl.multiple_of(k * quarter, quarter), quarter), :]
                )

    vmem = pl.BlockSpec(memory_space=pltpu.VMEM)
    shape = jax.ShapeDtypeStruct((count, quarter, width), F32)
    return pl.pallas_call(
        kernel,
        out_shape=[shape, shape],
        in_specs=[pl.BlockSpec(memory_space=pltpu.SMEM), vmem, vmem],
        out_specs=[vmem, vmem],
        compiler_params=pltpu.CompilerParams(vmem_limit_bytes=6 * MIB),
        cost_estimate=SHORT,
        name="fold",
    )(places, mine, got)


def merge(top, corner):
    size = top.shape[1]

    def kernel(top, corner, out):
        for c in range(2):
            out[c] = top[c] + corner[c, :size, :]

    vmem = pl.BlockSpec(memory_space=pltpu.VMEM)
    return pl.pallas_call(
        kernel,
        out_shape=jax.ShapeDtypeStruct(top.shape, F32),
        in_specs=[vmem, vmem],
        out_specs=vmem,
        compiler_params=pltpu.CompilerParams(vmem_limit_bytes=4 * MIB),
        cost_estimate=SHORT,
        name="merge",
    )(top, corner)


def annotate(lower, bottom):
    size = bottom.shape[2]

    def kernel(lower, bottom, out, sem):
        source = bottom.at[0, pl.ds(bottom.shape[1] - 8, 8)]
        copy = pltpu.make_async_copy(source, out.at[0, pl.ds(out.shape[1] - 8, 8), pl.ds(0, size)], sem.at[0])
        copy.start()
        copy.wait()

    anywhere = pl.BlockSpec(memory_space=pl.ANY)
    return pl.pallas_call(
        kernel,
        out_shape=jax.ShapeDtypeStruct(lower.shape, F32),
        in_specs=[anywhere, anywhere],
        out_specs=anywhere,
        input_output_aliases={0: 0},
        scratch_shapes=[pltpu.SemaphoreType.DMA((1,))],
        compiler_params=pltpu.CompilerParams(vmem_limit_bytes=MIB),
        cost_estimate=SHORT,
        name="annotate",
    )(lower, bottom)


def deal(terms, parts, rows):
    count, _, width = terms[0].shape
    if rows % 8:
        return sum(terms).reshape(count, parts, rows, width).transpose(1, 0, 2, 3)

    def kernel(*refs):
        terms, out = refs[:-1], refs[-1]
        for j in range(parts):
            for c in range(count):
                out[j, c] = sum(term[c, j * rows : (j + 1) * rows, :] for term in terms)

    vmem = pl.BlockSpec(memory_space=pltpu.VMEM)
    return pl.pallas_call(
        kernel,
        out_shape=jax.ShapeDtypeStruct((parts, count, rows, width), F32),
        in_specs=[vmem] * len(terms),
        out_specs=vmem,
        compiler_params=pltpu.CompilerParams(vmem_limit_bytes=4 * MIB),
        cost_estimate=SHORT,
        name="deal",
    )(*terms)


def settle(places, start, probe, pieces):
    parts, count, rows, width = pieces.shape
    shape = (parts, count - 1, rows, width)
    if rows % 8:
        share = pieces.sum(axis=0)
        old = lax.dynamic_slice_in_dim(probe, places[0, start], rows, axis=1)
        return jnp.broadcast_to((old + share[:-1] / (share[-1:] + 1.0))[None], shape)

    def kernel(places, probe, pieces, out, old, sem):
        spot = pl.ds(pl.multiple_of(places[0, start], 8), rows)
        copy = pltpu.make_async_copy(probe.at[:, spot], old, sem.at[0])
        copy.start()
        share = sum(pieces[j] for j in range(parts))
        copy.wait()
        new = old[...] + share[:-1] / (share[-1:] + 1.0)
        for j in range(parts):
            out[j] = new

    vmem = pl.BlockSpec(memory_space=pltpu.VMEM)
    return pl.pallas_call(
        kernel,
        out_shape=jax.ShapeDtypeStruct(shape, F32),
        in_specs=[pl.BlockSpec(memory_space=pltpu.SMEM), pl.BlockSpec(memory_space=pltpu.HBM), vmem],
        out_specs=vmem,
        scratch_shapes=[pltpu.VMEM(shape[1:], F32), pltpu.SemaphoreType.DMA((1,))],
        compiler_params=pltpu.CompilerParams(vmem_limit_bytes=4 * MIB),
        cost_estimate=SHORT,
        name="settle",
    )(places, in_hbm(probe), pieces)


def collect(pieces):
    parts, count, rows, width = pieces.shape
    if rows % 8:
        return pieces.transpose(1, 0, 2, 3).reshape(count, parts * rows, width)

    def kernel(pieces, out):
        for j in range(parts):
            for c in range(count):
                out[c, j * rows : (j + 1) * rows, :] = pieces[j, c]

    vmem = pl.BlockSpec(memory_space=pltpu.VMEM)
    return pl.pallas_call(
        kernel,
        out_shape=jax.ShapeDtypeStruct((count, parts * rows, width), F32),
        in_specs=[vmem],
        out_specs=vmem,
        compiler_params=pltpu.CompilerParams(vmem_limit_bytes=4 * MIB),
        cost_estimate=LONG,
        name="collect",
    )(pieces)


def join(places, upper, mine, other):
    half = mine.shape[1]

    def kernel(places, mine, other, out, sems):
        copies = [
            pltpu.make_async_copy(source, out.at[:, pl.ds(pl.multiple_of(at * half, half), half)], sems.at[i])
            for i, (source, at) in enumerate(((mine, places[0, upper]), (other, 1 - places[0, upper])))
        ]
        for copy in copies:
            copy.start()
        for copy in copies:
            copy.wait()

    anywhere = pl.BlockSpec(memory_space=pl.ANY)
    return pl.pallas_call(
        kernel,
        out_shape=jax.ShapeDtypeStruct((mine.shape[0], 2 * half) + mine.shape[2:], F32),
        in_specs=[pl.BlockSpec(memory_space=pltpu.SMEM), anywhere, anywhere],
        out_specs=anywhere,
        scratch_shapes=[pltpu.SemaphoreType.DMA((2,))],
        compiler_params=pltpu.CompilerParams(vmem_limit_bytes=MIB),
        cost_estimate=pl.CostEstimate(flops=0, bytes_accessed=2_000_000, transcendentals=0),
        name="join",
    )(places, mine, other)


def body(object_field, probe, amplitudes, positions, counts):
    modes, _, size, _ = probe.shape
    tile_rows, tile_cols = object_field.shape[1:]
    slots = amplitudes.shape[0]
    origin = jnp.stack([lax.axis_index("row") * tile_rows, lax.axis_index("col") * tile_cols]).astype(jnp.int32)
    bits = [1 << k for k in range(lax.axis_size("row").bit_length() - 1)]
    uppers = [(lax.axis_index("row") & bit) // bit for bit in bits]

    def relative(table):
        return jnp.concatenate([table[:, : 2 * slots] - jnp.tile(origin, slots)[None], table[:, 2 * slots :]], axis=1)

    right_up, right_down = cut(
        object_field, ((0, size, size), (size, tile_rows - size, size)), SHORT, "cut_right"
    )
    right_up, right_down, after_right = together(right_up, right_down, object_field)
    right_up = from_behind(right_up, "col", -1)
    right_down = from_behind(right_down, "col", -1)
    (lower,) = cut(after_right, ((0, size, tile_cols),), LONG, "cut_lower")
    meta = jnp.concatenate([positions.reshape(1, 2 * slots), counts.reshape(1, 1)], axis=1)
    lower = from_behind(lower, "row", -1)

    parts = lax.axis_size("col")
    rows = (size >> len(bits)) // parts
    me = lax.axis_index("col")
    start = sum(upper * (size >> (k + 1)) for k, upper in enumerate(uppers)) + me * rows
    bit_at = 2 * slots + 2
    me_at = bit_at + len(bits)
    start_at, origin_at = me_at + 1, me_at + 2
    extra = [1 - uppers[0], *uppers, me, start, origin[0], origin[1]]
    mine = jnp.concatenate([relative(meta), jnp.stack([item.astype(jnp.int32) for item in extra])[None]], axis=1)
    note = jnp.pad(meta.astype(F32), ((0, 7), (0, size - meta.shape[1])))
    mine, note = together(mine, note)
    amplitudes = arrange(mine, amplitudes)
    right_up, amplitudes = together(right_up, amplitudes)
    corner = from_behind(right_up, "row", -1)
    amplitudes, lower = together(amplitudes, lower)
    state = visit_inside(mine, probe, amplitudes, object_field, lower)
    right_up, right_down, corner, *state = together(right_up, right_down, corner, *state)
    own, bottom_spill, top_spill, corner_spill, lower_spill, send, share = visit_beyond(
        mine, probe, amplitudes, [right_up, right_down, corner], note, state
    )

    index = bit_at
    for k, bit in enumerate(bits):
        got = exchange(send, "row", bit)
        if k == 0:
            bottom_spill = from_behind(bottom_spill, "col", 1)
        if k + 1 < len(bits):
            send, share = fold(mine, index, share, got, bit_at + k + 1)
            index = None
    got, bottom_spill, lower_spill = together(got, bottom_spill, lower_spill)
    lower_spill = from_behind(annotate(lower_spill, bottom_spill), "row", 1)
    pieces = lax.all_to_all(deal([share, got], parts, rows), "col", 0, 0, tiled=True)
    new = settle(mine, start_at, probe.reshape(2 * modes, size, size), pieces)
    new, lower_spill, corner_spill = together(new, lower_spill, corner_spill)
    corner_spill = from_behind(corner_spill, "row", 1)
    inverse_light = light(
        mine, slots, origin_at, probe, bottom_spill, corner_spill, lower_spill, (tile_rows, tile_cols)
    )
    new = lax.all_to_all(new, "col", 0, 0, tiled=True)
    new, corner_spill = together(new, corner_spill)
    top_spill, new = together(merge(top_spill, corner_spill), new)
    top_spill = from_behind(top_spill, "col", 1)
    new = collect(new)
    for k, bit in reversed(list(enumerate(bits))):
        if k == 0:
            new, own = together(new, own)
            new_object = finish(own, None, bottom_spill, lower_spill, inverse_light, object_field)
            new_object, top_spill = together(new_object, top_spill)
            new_object = finish(
                own, top_spill, bottom_spill, lower_spill, inverse_light, object_field, before=new_object
            )
        other = exchange(new, "row", bit)
        if k + 1 == len(bits):
            other, inverse_light = together(other, inverse_light)
        if k == 0:
            other, new_object = together(other, new_object)
        new = join(mine, bit_at + k, new, other)
    return (new_object, new.reshape(modes, 2, size, size))


def solution(mesh):
    in_specs = (
        P(None, "row", "col"),
        P(),
        P(("row", "col"), None, None),
        P(("row", "col"), None),
        P(("row", "col")),
    )
    out_specs = (P(None, "row", "col"), P())
    return jax.shard_map(body, mesh=mesh, in_specs=in_specs, out_specs=out_specs, check_vma=False)
```

profile of v0, /device:TPU:0, one launch (start us, length us, event | category | flops | bytes accessed | tf_op | source)
XLA Modules:
  0.0 123.3 jit_solution(14527389690740675879)
XLA Ops:
  0.6 2.2 %cut_right.1 = (f32[2,256,256]{2,1,0:T(8,128)}, f32[2,256,256]{2,1,0:T(8,128)}) custom-call(f32[2,512,512]{2,1,0:T(8,128)} %tile.15), custom_call_target="tpu_custom_call" | custom-call | bytes 1000000 | tf_op jit(solution)/shard_map/cut_right/pallas_call | solution.py:705
  2.8 1.3 %collective-permute-start = (f32[2,256,256]{2,1,0:T(8,128)}, f32[2,256,256]{2,1,0:T(8,128)S(1)}, u32[]{:S(2)}, u32[]{:S(2)}) collective-permute-start(f32[2,256,256]{2,1,0:T(8,128)} %get-tuple-element.52), channel_id=1, source_target_pairs={{1,0},{2,1},{3,2},{4,3},{5,4},{6,5},{7,6},{9,8},{10,9},{11,10},{12... | collective-permute-start | bytes 1572872 | tf_op jit(solution)/shard_map/ppermute | solution.py:681
  4.1 1.3 %collective-permute-start.2 = (f32[2,256,256]{2,1,0:T(8,128)}, f32[2,256,256]{2,1,0:T(8,128)S(1)}, u32[]{:S(2)}, u32[]{:S(2)}) collective-permute-start(f32[2,256,256]{2,1,0:T(8,128)} %get-tuple-element.57), channel_id=1, source_target_pairs={{1,0},{2,1},{3,2},{4,3},{5,4},{6,5},{7,6},{9,8},{10,9},{11,10},{12... | collective-permute-start | bytes 1572872 | tf_op jit(solution)/shard_map/ppermute | solution.py:681
  5.4 1.2 %cut_lower.1 = f32[2,256,512]{2,1,0:T(8,128)S(1)} custom-call(f32[2,512,512]{2,1,0:T(8,128)} %tile.15), custom_call_target="tpu_custom_call" | custom-call | flops 30000001024 | bytes 4000000 | tf_op jit(solution)/shard_map/cut_lower/pallas_call | solution.py:705
  6.7 1.3 %collective-permute-start.1 = (f32[2,256,512]{2,1,0:T(8,128)S(1)}, f32[2,256,512]{2,1,0:T(8,128)S(1)}, u32[]{:S(2)}, u32[]{:S(2)}) collective-permute-start(f32[2,256,512]{2,1,0:T(8,128)S(1)} %cut_lower.1), channel_id=1, source_target_pairs={{8,0},{16,8},{24,16},{9,1},{17,9},{25,17},{10,2},{18,10},{26,18},{... | collective-permute-start | bytes 3145736 | tf_op jit(solution)/shard_map/ppermute | solution.py:681
  8.7 0.1 broadcast_in_dim_tile.3
  8.8 0.1 copy.17
  8.9 0.1 reshape.73
  9.1 0.1 stack.35
  9.2 3.6 %arrange.1.amplitudes = f32[8,256,256]{2,1,0:T(8,128)} custom-call(s32[1,24]{1,0:T(1,128)S(1)} %pad_add_fusion.1.meta.places, f32[8,256,256]{2,1,0:T(8,128)} %amplitudes.1), custom_call_target="tpu_custom_call" | custom-call | flops 30000001024 | bytes 4000000 | tf_op jit(solution)/shard_map/arrange/pallas_call | solution.py:244
  12.8 7.9 %collective-permute-done.refs_0_ = f32[2,256,256]{2,1,0:T(8,128)S(1)} collective-permute-done((f32[2,256,256]{2,1,0:T(8,128)}, f32[2,256,256]{2,1,0:T(8,128)S(1)}, u32[]{:S(2)}, u32[]{:S(2)}) %collective-permute-start) | collective-permute-done | bytes 524320 | tf_op jit(solution)/shard_map/ppermute | solution.py:681
  20.7 1.3 %collective-permute-start.3 = (f32[2,256,256]{2,1,0:T(8,128)S(1)}, f32[2,256,256]{2,1,0:T(8,128)S(1)}, u32[]{:S(2)}, u32[]{:S(2)}) collective-permute-start(f32[2,256,256]{2,1,0:T(8,128)S(1)} %collective-permute-done.refs_0_), channel_id=1, source_target_pairs={{8,0},{16,8},{24,16},{9,1},{17,9},{25,17},{10,2},{18,10},{26,18},{... | collective-permute-start | bytes 1572872 | tf_op jit(solution)/shard_map/ppermute | solution.py:681
  22.0 12.4 %slots_inside.1 = (f32[2,768,768]{2,1,0:T(8,128)S(1)}, f32[2,768,768]{2,1,0:T(8,128)S(1)}, f32[5,256,256]{2,1,0:T(8,128)S(1)}) custom-call(s32[1,24]{1,0:T(1,128)S(1)} %pad_add_fusion.1.meta.places, f32[2,2,256,256]{3,2,1,0:T(8,128)S(1)} %copy-done, f32[8,256,256]{2,1,0:T(8,128)} %arrange.1.amplitudes, f32[2,512,512]{2,1,0:T(8,128)} %tile.15, ...), custom_call_target="tpu_custom_call" | custom-call | flops 12000000000 | bytes 16000000 | tf_op jit(solution)/shard_map/slots_inside/pallas_call | solution.py:544
  34.4 7.1 %slots_beyond.1 = (f32[2,768,768]{2,1,0:T(8,128)S(1)}, f32[2,768,768]{2,1,0:T(8,128)S(1)}, f32[5,256,256]{2,1,0:T(8,128)S(1)}, f32[2,512,512]{2,1,0:T(8,128)}, f...) custom-call(s32[1,24]{1,0:T(1,128)S(1)} %pad_add_fusion.1.meta.place, ...), custom_call_target="tpu_custom_call", output_to_operand_aliasing={{0}: (9, {}), {1}: (10, {}), {2}: (11, {})} | custom-call | flops 12000000000 | bytes 16000000 | tf_op jit(solution)/shard_map/slots_beyond/pallas_call | solution.py:576
  41.5 2.5 %collective-permute-start.4 = (f32[5,128,256]{2,1,0:T(8,128)S(1)}, f32[5,128,256]{2,1,0:T(8,128)S(1)}, u32[]{:S(2)}, u32[]{:S(2)}) collective-permute-start(f32[5,128,256]{2,1,0:T(8,128)S(1)} %get-tuple-element.71), channel_id=1, source_target_pairs={{0,8},{8,0},{16,24},{24,16},{1,9},{9,1},{17,25},{25,17},{2,10},{10... | collective-permute-start | bytes 1966088 | tf_op jit(solution)/shard_map/ppermute | solution.py:686
  44.0 5.2 %collective-permute-start.6 = (f32[2,264,256]{2,1,0:T(8,128)S(1)}, f32[2,264,256]{2,1,0:T(8,128)S(1)}, u32[]{:S(2)}, u32[]{:S(2)}) collective-permute-start(f32[2,264,256]{2,1,0:T(8,128)S(1)} %get-tuple-element.74), channel_id=1, source_target_pairs={{0,1},{1,2},{2,3},{3,4},{4,5},{5,6},{6,7},{8,9},{9,10},{10,11},{11... | collective-permute-start | bytes 1622024 | tf_op jit(solution)/shard_map/ppermute | solution.py:681
  49.3 0.6 fold.1
  49.9 1.4 %collective-permute-start.5 = (f32[5,64,256]{2,1,0:T(8,128)S(1)}, f32[5,64,256]{2,1,0:T(8,128)S(1)}, u32[]{:S(2)}, u32[]{:S(2)}) collective-permute-start(f32[5,64,256]{2,1,0:T(8,128)S(1)} %get-tuple-element.73), channel_id=1, source_target_pairs={{0,16},{8,24},{16,0},{24,8},{1,17},{9,25},{17,1},{25,9},{2,18},{10... | collective-permute-start | bytes 983048 | tf_op jit(solution)/shard_map/ppermute | solution.py:686
  51.3 9.9 %collective-permute-done.6.bottom = f32[2,264,256]{2,1,0:T(8,128)S(1)} collective-permute-done((f32[2,264,256]{2,1,0:T(8,128)S(1)}, f32[2,264,256]{2,1,0:T(8,128)S(1)}, u32[]{:S(2)}, u32[]{:S(2)}) %collective-permute-start.6) | collective-permute-done | bytes 540704 | tf_op jit(solution)/shard_map/ppermute | solution.py:681
  61.3 1.5 %collective-permute-start.7 = (f32[2,264,512]{2,1,0:T(8,128)S(1)}, f32[2,264,512]{2,1,0:T(8,128)S(1)}, u32[]{:S(2)}, u32[]{:S(2)}) collective-permute-start(f32[2,264,512]{2,1,0:T(8,128)S(1)} %annotate.1), channel_id=1, source_target_pairs={{0,8},{8,16},{16,24},{1,9},{9,17},{17,25},{2,10},{10,18},{18,26},{... | collective-permute-start | bytes 3244040 | tf_op jit(solution)/shard_map/ppermute | solution.py:681
  62.8 28.8 %all_to_all.10.pieces = f32[8,5,8,256]{3,2,1,0:T(8,128)S(1)} all-to-all(f32[8,5,8,256]{3,2,1,0:T(8,128)S(1)} %deal.1), channel_id=1, replica_groups=mesh['row'=4,'col'=8] {'col'}, dimensions={0} | all-to-all | bytes 655360 | tf_op jit(solution)/shard_map/all_to_all | solution.py:939
  91.6 1.3 %settle.1 = f32[8,4,8,256]{3,2,1,0:T(8,128)S(1)} custom-call(s32[1,24]{1,0:T(1,128)S(1)} %pad_add_fusion.1.meta.places, f32[4,256,256]{2,1,0:T(8,128)} %bitcast.13, f32[8,5,8,256]{3,2,1,0:T(8,128)S(1)} %all_to_all.10.pieces), custom_call_target="tpu_custom_call" | custom-call | bytes 1000000 | tf_op jit(solution)/shard_map/settle/pallas_call | solution.py:827
  93.0 1.3 %collective-permute-start.8 = (f32[2,264,256]{2,1,0:T(8,128)S(1)}, f32[2,264,256]{2,1,0:T(8,128)S(1)}, u32[]{:S(2)}, u32[]{:S(2)}) collective-permute-start(f32[2,264,256]{2,1,0:T(8,128)S(1)} %get-tuple-element.81), channel_id=1, source_target_pairs={{0,8},{8,16},{16,24},{1,9},{9,17},{17,25},{2,10},{10,18},{18,26},{... | collective-permute-start | bytes 1622024 | tf_op jit(solution)/shard_map/ppermute | solution.py:681
  94.3 12.0 %all_to_all.11.pieces = f32[8,4,8,256]{3,2,1,0:T(8,128)S(1)} all-to-all(f32[8,4,8,256]{3,2,1,0:T(8,128)S(1)} %settle.1), channel_id=1, replica_groups=mesh['row'=4,'col'=8] {'col'}, dimensions={0} | all-to-all | bytes 524288 | tf_op jit(solution)/shard_map/all_to_all | solution.py:946
  106.3 0.1 merge.1
  106.5 3.4 %collective-permute-start.11 = (f32[2,256,256]{2,1,0:T(8,128)S(1)}, f32[2,256,256]{2,1,0:T(8,128)S(1)}, u32[]{:S(2)}, u32[]{:S(2)}) collective-permute-start(f32[2,256,256]{2,1,0:T(8,128)S(1)} %merge.1), channel_id=1, source_target_pairs={{0,1},{1,2},{2,3},{3,4},{4,5},{5,6},{6,7},{8,9},{9,10},{10,11},{11... | collective-permute-start | bytes 1572872 | tf_op jit(solution)/shard_map/ppermute | solution.py:681
  109.9 3.2 %light.1.scale = f32[512,512]{1,0:T(8,128)S(1)} custom-call(s32[1,24]{1,0:T(1,128)S(1)} %pad_add_fusion.1.meta.places, f32[2,2,256,256]{3,2,1,0:T(8,128)} %probe_h.1, f32[2,264,256]{2,1,0:T(8,128)S(1)} %collective-permute-done.6.bottom, f32[2,264,256]{2,1,0:T(8,128)S(1)} %collective-permute-done.8.corner, f32[2,264,512]{2,1,0:T(8,128)S(1)} %collective-permute-done.7.lower), custom_call_target="tpu_custom_call" | custom-call | flops 4000000000 | bytes 1000000 | tf_op jit(solution)/shard_map/light/pallas_call | solution.py:177
  113.1 0.6 join.2.mine
  113.8 2.6 %finish_far.1.before = f32[2,512,512]{2,1,0:T(8,128)} custom-call(f32[2,512,512]{2,1,0:T(8,128)} %get-tuple-element.89.own, f32[2,264,256]{2,1,0:T(8,128)S(1)} %collective-permute-done.6.bottom, f32[512,512]{1,0:T(8,128)S(1)} %light.1.scale, f32[2,512,512]{2,1,0:T(8,128)} %tile.15), custom_call_target="tpu_custom_call" | custom-call | flops 2000000000 | bytes 6000000 | tf_op jit(solution)/shard_map/finish_far/pallas_call | solution.py:657
  116.4 2.5 %collective-permute-done.11.top = f32[2,256,256]{2,1,0:T(8,128)S(1)} collective-permute-done((f32[2,256,256]{2,1,0:T(8,128)S(1)}, f32[2,256,256]{2,1,0:T(8,128)S(1)}, u32[]{:S(2)}, u32[]{:S(2)}) %collective-permute-start.11) | collective-permute-done | bytes 524320 | tf_op jit(solution)/shard_map/ppermute | solution.py:681
  118.9 2.6 %finish_near.1 = f32[2,512,512]{2,1,0:T(8,128)} custom-call(f32[2,512,512]{2,1,0:T(8,128)} %finish_far.1.before, f32[2,512,512]{2,1,0:T(8,128)} %get-tuple-element.89.own, f32[2,256,256]{2,1,0:T(8,128)S(1)} %collective-permute-done.11.top, f32[2,264,512]{2,1,0:T(8,128)S(1)} %collective-permute-done.7.lower, ...), custom_call_target="tpu_custom_call", output_to_operand_aliasing={{}: (0, {})} | custom-call | flops 2000000000 | bytes 6000000 | tf_op jit(solution)/shard_map/finish_near/pallas_call | solution.py:657
  121.6 1.5 %join.3 = f32[4,256,256]{2,1,0:T(8,128)} custom-call(s32[1,24]{1,0:T(1,128)S(1)} %pad_add_fusion.1.meta.places, f32[4,128,256]{2,1,0:T(8,128)S(1)} %join.2.mine, f32[4,128,256]{2,1,0:T(8,128)S(1)} %collective-permute-done.10.other), custom_call_target="tpu_custom_call" | custom-call | bytes 2000000 | tf_op jit(solution)/shard_map/join/pallas_call | solution.py:875
  (24 shorter events, 0.5 us)
Async XLA Ops:
  2.8 6.0 %copy-start.1 = (s32[8,2]{0,1:T(2,128)S(1)}, s32[8,2]{0,1:T(2,128)}, u32[]{:S(2)}) copy-start(s32[8,2]{0,1:T(2,128)} %param.12) | copy-start | bytes 196
  2.8 17.8 %collective-permute-start = (f32[2,256,256]{2,1,0:T(8,128)}, f32[2,256,256]{2,1,0:T(8,128)S(1)}, u32[]{:S(2)}, u32[]{:S(2)}) collective-permute-start(f32[2,256,256]{2,1,0:T(8,128)} %get-tuple-element.52), channel_id=1, source_target_pairs={{1,0},{2,1},{3,2},{4,3},{5,4},{6,5},{7,6},{9,8},{10,9},{11,10},{12... | collective-permute-start | bytes 1572872 | tf_op jit(solution)/shard_map/ppermute | solution.py:681
  4.1 30.2 %collective-permute-start.2 = (f32[2,256,256]{2,1,0:T(8,128)}, f32[2,256,256]{2,1,0:T(8,128)S(1)}, u32[]{:S(2)}, u32[]{:S(2)}) collective-permute-start(f32[2,256,256]{2,1,0:T(8,128)} %get-tuple-element.57), channel_id=1, source_target_pairs={{1,0},{2,1},{3,2},{4,3},{5,4},{6,5},{7,6},{9,8},{10,9},{11,10},{12... | collective-permute-start | bytes 1572872 | tf_op jit(solution)/shard_map/ppermute | solution.py:681
  6.7 15.3 %collective-permute-start.1 = (f32[2,256,512]{2,1,0:T(8,128)S(1)}, f32[2,256,512]{2,1,0:T(8,128)S(1)}, u32[]{:S(2)}, u32[]{:S(2)}) collective-permute-start(f32[2,256,512]{2,1,0:T(8,128)S(1)} %cut_lower.1), channel_id=1, source_target_pairs={{8,0},{16,8},{24,16},{9,1},{17,9},{25,17},{10,2},{18,10},{26,18},{... | collective-permute-start | bytes 3145736 | tf_op jit(solution)/shard_map/ppermute | solution.py:681
  9.2 12.7 %copy-start = (f32[2,2,256,256]{3,2,1,0:T(8,128)S(1)}, f32[2,2,256,256]{3,2,1,0:T(8,128)}, u32[]{:S(2)}) copy-start(f32[2,2,256,256]{3,2,1,0:T(8,128)} %probe_h.1) | copy-start | bytes 3145732
  20.7 13.7 %collective-permute-start.3 = (f32[2,256,256]{2,1,0:T(8,128)S(1)}, f32[2,256,256]{2,1,0:T(8,128)S(1)}, u32[]{:S(2)}, u32[]{:S(2)}) collective-permute-start(f32[2,256,256]{2,1,0:T(8,128)S(1)} %collective-permute-done.refs_0_), channel_id=1, source_target_pairs={{8,0},{16,8},{24,16},{9,1},{17,9},{25,17},{10,2},{18,10},{26,18},{... | collective-permute-start | bytes 1572872 | tf_op jit(solution)/shard_map/ppermute | solution.py:681
  41.5 7.7 %collective-permute-start.4 = (f32[5,128,256]{2,1,0:T(8,128)S(1)}, f32[5,128,256]{2,1,0:T(8,128)S(1)}, u32[]{:S(2)}, u32[]{:S(2)}) collective-permute-start(f32[5,128,256]{2,1,0:T(8,128)S(1)} %get-tuple-element.71), channel_id=1, source_target_pairs={{0,8},{8,0},{16,24},{24,16},{1,9},{9,1},{17,25},{25,17},{2,10},{10... | collective-permute-start | bytes 1966088 | tf_op jit(solution)/shard_map/ppermute | solution.py:686
  44.0 17.2 %collective-permute-start.6 = (f32[2,264,256]{2,1,0:T(8,128)S(1)}, f32[2,264,256]{2,1,0:T(8,128)S(1)}, u32[]{:S(2)}, u32[]{:S(2)}) collective-permute-start(f32[2,264,256]{2,1,0:T(8,128)S(1)} %get-tuple-element.74), channel_id=1, source_target_pairs={{0,1},{1,2},{2,3},{3,4},{4,5},{5,6},{6,7},{8,9},{9,10},{10,11},{11... | collective-permute-start | bytes 1622024 | tf_op jit(solution)/shard_map/ppermute | solution.py:681
  49.9 11.4 %collective-permute-start.5 = (f32[5,64,256]{2,1,0:T(8,128)S(1)}, f32[5,64,256]{2,1,0:T(8,128)S(1)}, u32[]{:S(2)}, u32[]{:S(2)}) collective-permute-start(f32[5,64,256]{2,1,0:T(8,128)S(1)} %get-tuple-element.73), channel_id=1, source_target_pairs={{0,16},{8,24},{16,0},{24,8},{1,17},{9,25},{17,1},{25,9},{2,18},{10... | collective-permute-start | bytes 983048 | tf_op jit(solution)/shard_map/ppermute | solution.py:686
  61.3 31.7 %collective-permute-start.7 = (f32[2,264,512]{2,1,0:T(8,128)S(1)}, f32[2,264,512]{2,1,0:T(8,128)S(1)}, u32[]{:S(2)}, u32[]{:S(2)}) collective-permute-start(f32[2,264,512]{2,1,0:T(8,128)S(1)} %annotate.1), channel_id=1, source_target_pairs={{0,8},{8,16},{16,24},{1,9},{9,17},{17,25},{2,10},{10,18},{18,26},{... | collective-permute-start | bytes 3244040 | tf_op jit(solution)/shard_map/ppermute | solution.py:681
  93.0 13.4 %collective-permute-start.8 = (f32[2,264,256]{2,1,0:T(8,128)S(1)}, f32[2,264,256]{2,1,0:T(8,128)S(1)}, u32[]{:S(2)}, u32[]{:S(2)}) collective-permute-start(f32[2,264,256]{2,1,0:T(8,128)S(1)} %get-tuple-element.81), channel_id=1, source_target_pairs={{0,8},{8,16},{16,24},{1,9},{9,17},{17,25},{2,10},{10,18},{18,26},{... | collective-permute-start | bytes 1622024 | tf_op jit(solution)/shard_map/ppermute | solution.py:681
  106.4 6.6 %collective-permute-start.9 = (f32[4,64,256]{2,1,0:T(8,128)S(1)}, f32[4,64,256]{2,1,0:T(8,128)S(1)}, u32[]{:S(2)}, u32[]{:S(2)}) collective-permute-start(f32[4,64,256]{2,1,0:T(8,128)S(1)} %collect.1.mine), channel_id=1, source_target_pairs={{0,16},{8,24},{16,0},{24,8},{1,17},{9,25},{17,1},{25,9},{2,18},{10... | collective-permute-start | bytes 786440 | tf_op jit(solution)/shard_map/ppermute | solution.py:686
  106.5 12.4 %collective-permute-start.11 = (f32[2,256,256]{2,1,0:T(8,128)S(1)}, f32[2,256,256]{2,1,0:T(8,128)S(1)}, u32[]{:S(2)}, u32[]{:S(2)}) collective-permute-start(f32[2,256,256]{2,1,0:T(8,128)S(1)} %merge.1), channel_id=1, source_target_pairs={{0,1},{1,2},{2,3},{3,4},{4,5},{5,6},{6,7},{8,9},{9,10},{10,11},{11... | collective-permute-start | bytes 1572872 | tf_op jit(solution)/shard_map/ppermute | solution.py:681
  113.7 7.9 %collective-permute-start.10 = (f32[4,128,256]{2,1,0:T(8,128)S(1)}, f32[4,128,256]{2,1,0:T(8,128)S(1)}, u32[]{:S(2)}, u32[]{:S(2)}) collective-permute-start(f32[4,128,256]{2,1,0:T(8,128)S(1)} %join.2.mine), channel_id=1, source_target_pairs={{0,8},{8,0},{16,24},{24,16},{1,9},{9,1},{17,25},{25,17},{2,10},{10... | collective-permute-start | bytes 1572872 | tf_op jit(solution)/shard_map/ppermute | solution.py:686
where the time goes:
time: 125 us; the launch traced here: 123 us
  blocking collectives  40.8 us (33%)
  Pallas kernels  39.2 us (31%)
  starting transfers between devices  20.6 us (16%)
  waiting for transfers between devices  20.3 us (16%)
  between operations  1.71 us (1%)
    all_to_all x1, blocking collectives, body(): lax.all_to_all(deal([share, got], parts, rows), 'col', 0, 0, tiled=True)  28.8 us
    ppermute x8, waiting for transfers between devices, from_behind(): return lax.ppermute(array, axis, pairs)  20.3 us
    ppermute x8, starting transfers between devices, from_behind(): return lax.ppermute(array, axis, pairs)  16.6 us
    pallas_call x1, Pallas kernels, visit_inside(): pl.pallas_call(kernel, out_shape=[field, field, pltpu.VMEM((2 * modes + 1...  12.4 us
    all_to_all x1, blocking collectives, body(): new = lax.all_to_all(new, 'col', 0, 0, tiled=True)  12 us
    pallas_call x1, Pallas kernels, visit_beyond(): pl.pallas_call(kernel, out_shape=[pltpu.VMEM(item.shape, item.dtype) for...  7.13 us
    pallas_call x2, Pallas kernels, finish(): pl.pallas_call(kernel, out_shape=pltpu.HBM(tile.shape, F32), in_specs=in_...  5.26 us
    ppermute x4, starting transfers between devices, exchange(): return lax.ppermute(array, axis, [(i, i ^ bit) for i in range(count)])  4.04 us
  transfers between devices with their start and end apart: 12, of which 3 were waited for; matrix products, arithmetic and copies ran while one was open for 0% of the time, Pallas kernels for 23%

commit v1 on v0

--- a/solution.py
+++ b/solution.py
@@ -187,7 +187,7 @@
             pltpu.SemaphoreType.DMA((4,)),
         ],
         compiler_params=pltpu.CompilerParams(vmem_limit_bytes=8 * MIB),
-        cost_estimate=pl.CostEstimate(flops=4_000_000_000, bytes_accessed=1_000_000, transcendentals=0),
+        cost_estimate=pl.CostEstimate(flops=4_000_000_000, bytes_accessed=4_000_000, transcendentals=0),
         name="light",
     )(meta, in_hbm(probe), bottom, corner, lower)
 
@@ -589,9 +589,7 @@
     return (*out[3:], out[2])
 
 
-def finish_kernel(
-    chosen, own, top, bottom, lower, scale, tile, out, own_s, right_s, lower_s, scale_s, tile_s, in_sems, out_sems
-):
+def finish_far_kernel(own, bottom, lower, scale, tile, out, own_s, right_s, lower_s, scale_s, tile_s, in_sems, out_sems):
     size = right_s.shape[2]
     block = 128
     blocks = own_s.shape[1] // block
@@ -604,27 +602,28 @@
             (tile.at[:, rows], tile_s.at[:, rows]),
         ]
         if i < size // block:
-            pairs.append((top.at[:, rows], right_s.at[:, rows]))
             pairs.append((lower.at[:, rows], lower_s.at[:, rows]))
         else:
-            pairs.append((bottom.at[:, pl.ds(i * block - size, block)], right_s.at[:, rows]))
+            pairs.append((bottom.at[:, pl.ds(i * block - size, block)], right_s.at[:, pl.ds(i * block - size, block)]))
         return [pltpu.make_async_copy(a, b, in_sems.at[i, k]) for k, (a, b) in enumerate(pairs)]
 
-    loads = {i: copies(i) for i in range(blocks) if chosen(i * block)}
-    for load in loads.values():
+    loads = [copies(i) for i in range(blocks)]
+    for load in loads:
         for copy in load:
             copy.start()
     stores = []
-    for i in loads:
+    for i in range(blocks):
         for copy in loads[i]:
             copy.wait()
         rows = pl.ds(i * block, block)
         for at in range(i * block, (i + 1) * block, 32):
             part = pl.ds(at, 32)
             for c in range(2):
-                near, far = own_s[c, part, :size] + right_s[c, part, :], own_s[c, part, size:]
+                near, far = own_s[c, part, :size], own_s[c, part, size:]
                 if i < size // block:
                     near, far = near + lower_s[c, part, :size], far + lower_s[c, part, size:]
+                else:
+                    near = near + right_s[c, pl.ds(at - size, 32), :]
                 own_s[c, part, :size] = tile_s[c, part, :size] + near * scale_s[part, :size]
                 own_s[c, part, size:] = tile_s[c, part, size:] + far * scale_s[part, size:]
         stores.append(pltpu.make_async_copy(own_s.at[:, rows], out.at[:, rows], out_sems.at[i]))
@@ -633,46 +632,72 @@
         store.wait()
 
 
-def finish(own, top, bottom, lower, inverse_light, tile, before=None):
+def finish_far(own, bottom, lower, inverse_light, tile):
     rows, cols = tile.shape[1:]
     size = bottom.shape[2]
     anywhere = pl.BlockSpec(memory_space=pl.ANY)
     hbm = pl.BlockSpec(memory_space=pltpu.HBM)
-    if before is None:
-
-        def kernel(own, bottom, scale, tile, *refs):
-            finish_kernel(lambda at: at >= size, own, None, bottom, None, scale, tile, *refs)
-
-        operands = (in_hbm(own), bottom, inverse_light, in_hbm(tile))
-        in_specs = [hbm, anywhere, anywhere, hbm]
-        aliases = {}
-    else:
-
-        def kernel(before, own, top, lower, scale, tile, *refs):
-            finish_kernel(lambda at: at < size, own, top, None, lower, scale, tile, *refs)
-
-        operands = (in_hbm(before), in_hbm(own), top, lower, inverse_light, in_hbm(tile))
-        in_specs = [hbm, hbm, anywhere, anywhere, anywhere, hbm]
-        aliases = {0: 0}
-    return pl.pallas_call(
-        kernel,
+    return pl.pallas_call(
+        finish_far_kernel,
         out_shape=pltpu.HBM(tile.shape, F32),
-        in_specs=in_specs,
+        in_specs=[hbm, anywhere, anywhere, anywhere, hbm],
         out_specs=hbm,
-        input_output_aliases=aliases,
         scratch_shapes=[
             pltpu.VMEM(tile.shape, F32),
-            pltpu.VMEM((2, rows, size), F32),
+            pltpu.VMEM((2, rows - size, size), F32),
             pltpu.VMEM((2, size, cols), F32),
             pltpu.VMEM((rows, cols), F32),
             pltpu.VMEM(tile.shape, F32),
-            pltpu.SemaphoreType.DMA((rows // 128, 5)),
+            pltpu.SemaphoreType.DMA((rows // 128, 4)),
             pltpu.SemaphoreType.DMA((rows // 128,)),
         ],
         compiler_params=pltpu.CompilerParams(vmem_limit_bytes=12 * MIB),
-        cost_estimate=pl.CostEstimate(flops=2_000_000_000, bytes_accessed=6_000_000, transcendentals=0),
-        name="finish_far" if before is None else "finish_near",
-    )(*operands)
+        cost_estimate=pl.CostEstimate(flops=2_000_000_000, bytes_accessed=4_000_000, transcendentals=0),
+        name="finish_far",
+    )(in_hbm(own), bottom, lower, inverse_light, in_hbm(tile))
+
+
+def finish_near(before, top, inverse_light):
+    size = top.shape[2]
+
+    def kernel(before, top, scale, out, top_s, scale_s, out_s, sems, out_sems):
+        corner = (pl.ds(0, size), pl.ds(0, size))
+        loads = [
+            pltpu.make_async_copy(before.at[(slice(None), *corner)], out_s, sems.at[0]),
+            pltpu.make_async_copy(scale.at[corner], scale_s, sems.at[1]),
+            pltpu.make_async_copy(top, top_s, sems.at[2]),
+        ]
+        for load in loads:
+            load.start()
+        for load in loads:
+            load.wait()
+        stores = []
+        for c in range(2):
+            out_s[c] += top_s[c] * scale_s[...]
+            stores.append(pltpu.make_async_copy(out_s.at[c], out.at[(c, *corner)], out_sems.at[c]))
+            stores[-1].start()
+        for store in stores:
+            store.wait()
+
+    anywhere = pl.BlockSpec(memory_space=pl.ANY)
+    hbm = pl.BlockSpec(memory_space=pltpu.HBM)
+    return pl.pallas_call(
+        kernel,
+        out_shape=pltpu.HBM(before.shape, F32),
+        in_specs=[hbm, anywhere, anywhere],
+        out_specs=hbm,
+        input_output_aliases={0: 0},
+        scratch_shapes=[
+            pltpu.VMEM((2, size, size), F32),
+            pltpu.VMEM((size, size), F32),
+            pltpu.VMEM((2, size, size), F32),
+            pltpu.SemaphoreType.DMA((3,)),
+            pltpu.SemaphoreType.DMA((2,)),
+        ],
+        compiler_params=pltpu.CompilerParams(vmem_limit_bytes=4 * MIB),
+        cost_estimate=pl.CostEstimate(flops=2_000_000_000, bytes_accessed=4_000_000, transcendentals=0),
+        name="finish_near",
+    )(in_hbm(before), top, inverse_light)
 
 
 def from_behind(array, axis, by):
@@ -853,7 +878,7 @@
         in_specs=[vmem],
         out_specs=vmem,
         compiler_params=pltpu.CompilerParams(vmem_limit_bytes=4 * MIB),
-        cost_estimate=LONG,
+        cost_estimate=pl.CostEstimate(flops=30_000_000_000, bytes_accessed=4_000_000, transcendentals=0),
         name="collect",
     )(pieces)
 
@@ -934,32 +959,29 @@
         if k + 1 < len(bits):
             send, share = fold(mine, index, share, got, bit_at + k + 1)
             index = None
-    got, bottom_spill, lower_spill = together(got, bottom_spill, lower_spill)
-    lower_spill = from_behind(annotate(lower_spill, bottom_spill), "row", 1)
     pieces = lax.all_to_all(deal([share, got], parts, rows), "col", 0, 0, tiled=True)
     new = settle(mine, start_at, probe.reshape(2 * modes, size, size), pieces)
-    new, lower_spill, corner_spill = together(new, lower_spill, corner_spill)
+    new, bottom_spill, lower_spill, corner_spill = together(new, bottom_spill, lower_spill, corner_spill)
     corner_spill = from_behind(corner_spill, "row", 1)
-    inverse_light = light(
-        mine, slots, origin_at, probe, bottom_spill, corner_spill, lower_spill, (tile_rows, tile_cols)
-    )
+    lower_spill = from_behind(annotate(lower_spill, bottom_spill), "row", 1)
     new = lax.all_to_all(new, "col", 0, 0, tiled=True)
     new, corner_spill = together(new, corner_spill)
     top_spill, new = together(merge(top_spill, corner_spill), new)
     top_spill = from_behind(top_spill, "col", 1)
     new = collect(new)
+    inverse_light = light(
+        mine, slots, origin_at, probe, bottom_spill, corner_spill, lower_spill, (tile_rows, tile_cols)
+    )
     for k, bit in reversed(list(enumerate(bits))):
         if k == 0:
             new, own = together(new, own)
-            new_object = finish(own, None, bottom_spill, lower_spill, inverse_light, object_field)
-            new_object, top_spill = together(new_object, top_spill)
-            new_object = finish(
-                own, top_spill, bottom_spill, lower_spill, inverse_light, object_field, before=new_object
-            )
+            new_object = finish_far(own, bottom_spill, lower_spill, inverse_light, object_field)
         other = exchange(new, "row", bit)
         if k + 1 == len(bits):
             other, inverse_light = together(other, inverse_light)
         if k == 0:
+            new_object, top_spill = together(new_object, top_spill)
+            new_object = finish_near(new_object, top_spill, inverse_light)
             other, new_object = together(other, new_object)
         new = join(mine, bit_at + k, new, other)
     return (new_object, new.reshape(modes, 2, size, size))

time: 125 us -> 131 us (1.048)
  blocking collectives: 40.8 us -> 0 us
  starting transfers between devices: 20.6 us -> 52.1 us
  waiting for transfers between devices: 20.3 us -> 39.2 us
  Pallas kernels: 39.2 us -> 32.8 us
  local copies, waits for them, and re-layouts: 0.35 us -> 3.23 us
    all_to_all x2 -> x0, blocking collectives: 40.8 us -> none  [the longest x1 28.8 us: body(): lax.all_to_all(deal([share, got], parts, rows), 'col', 0, 0, tiled=True)]
    all_to_all x0 -> x2, starting transfers between devices: none -> 25.6 us  [the longest x1 17.8 us: body(): lax.all_to_all(deal([share, got], parts, rows), 'col', 0, 0, tiled=True)]
    ppermute x4, waiting for transfers between devices: 0.01 us -> 14.9 us  [exchange(): return lax.ppermute(array, axis, [(i, i ^ bit) for i in range(count)])]
    all_to_all x0 -> x2, waiting for transfers between devices: none -> 11.4 us  [the longest x1 6.05 us: body(): lax.all_to_all(deal([share, got], parts, rows), 'col', 0, 0, tiled=True)]
    ppermute x8, waiting for transfers between devices: 20.3 us -> 12.9 us  [from_behind(): return lax.ppermute(array, axis, pairs)]
    ppermute x4, starting transfers between devices: 4.04 us -> 10.1 us  [exchange(): return lax.ppermute(array, axis, [(i, i ^ bit) for i in range(count)])]
    pallas_call x1, Pallas kernels: 7.13 us -> 3.52 us  [visit_beyond(): pl.pallas_call(kernel, out_shape=[pltpu.VMEM(item.shape, item.dtype) for...]
    pallas_call x1, Pallas kernels: 12.4 us -> 9.27 us  [visit_inside(): pl.pallas_call(kernel, out_shape=[field, field, pltpu.VMEM((2 * modes + 1...]
  transfers between devices with their start and end apart: 12 -> 14, of which waited for: 3 -> 7; matrix products, arithmetic and copies ran while one was open for 0% -> 0% of each run, Pallas kernels for 23% -> 19%
where the time goes in v1:
time: 131 us; the launch traced here: 129 us
  starting transfers between devices  52.1 us (40%)
  waiting for transfers between devices  39.2 us (30%)
  Pallas kernels  32.8 us (25%)
  local copies, waits for them, and re-layouts  3.23 us (2%)
  between operations  1.72 us (1%)
    all_to_all x1, starting transfers between devices, body(): lax.all_to_all(deal([share, got], parts, rows), 'col', 0, 0, tiled=True)  17.8 us
    ppermute x8, starting transfers between devices, from_behind(): return lax.ppermute(array, axis, pairs)  16.4 us
    ppermute x4, waiting for transfers between devices, exchange(): return lax.ppermute(array, axis, [(i, i ^ bit) for i in range(count)])  14.9 us
    ppermute x8, waiting for transfers between devices, from_behind(): return lax.ppermute(array, axis, pairs)  12.9 us
    ppermute x4, starting transfers between devices, exchange(): return lax.ppermute(array, axis, [(i, i ^ bit) for i in range(count)])  10.1 us
    pallas_call x1, Pallas kernels, visit_inside(): pl.pallas_call(kernel, out_shape=[field, field, pltpu.VMEM((2 * modes + 1...  9.27 us
    all_to_all x1, starting transfers between devices, body(): new = lax.all_to_all(new, 'col', 0, 0, tiled=True)  7.75 us
    all_to_all x1, waiting for transfers between devices, body(): lax.all_to_all(deal([share, got], parts, rows), 'col', 0, 0, tiled=True)  6.05 us
  transfers between devices with their start and end apart: 14, of which 7 were waited for; matrix products, arithmetic and copies ran while one was open for 0% of the time, Pallas kernels for 19%

profile of v1, /device:TPU:0, one launch (start us, length us, event | category | flops | bytes accessed | tf_op | source)
XLA Modules:
  0.0 129.3 jit_solution(12286164877605710927)
XLA Ops:
  0.6 2.2 %cut_right.1 = (f32[2,256,256]{2,1,0:T(8,128)}, f32[2,256,256]{2,1,0:T(8,128)}) custom-call(f32[2,512,512]{2,1,0:T(8,128)} %tile.13), custom_call_target="tpu_custom_call" | custom-call | bytes 1000000 | tf_op jit(solution)/shard_map/cut_right/pallas_call | solution.py:730
  2.9 1.3 collective-permute-start
  4.2 1.3 collective-permute-start.2
  5.5 1.2 cut_lower.1
  6.7 1.3 collective-permute-start.1
  9.3 3.0 %arrange.1.amplitudes = f32[8,256,256]{2,1,0:T(8,128)} custom-call(s32[1,24]{1,0:T(1,128)S(1)} %pad_add_fusion.1.meta.places, f32[8,256,256]{2,1,0:T(8,128)} %amplitudes.1), custom_call_target="tpu_custom_call" | custom-call | flops 30000001024 | bytes 4000000 | tf_op jit(solution)/shard_map/arrange/pallas_call | solution.py:244
  12.3 8.4 %collective-permute-done.refs_0_ = f32[2,256,256]{2,1,0:T(8,128)S(1)} collective-permute-done((f32[2,256,256]{2,1,0:T(8,128)}, f32[2,256,256]{2,1,0:T(8,128)S(1)}, u32[]{:S(2)}, u32[]{:S(2)}) %collective-permute-start) | collective-permute-done | bytes 524320 | tf_op jit(solution)/shard_map/ppermute | solution.py:706
  20.7 1.3 collective-permute-start.3
  22.0 9.3 %slots_inside.1 = (f32[2,768,768]{2,1,0:T(8,128)S(1)}, f32[2,768,768]{2,1,0:T(8,128)S(1)}, f32[5,256,256]{2,1,0:T(8,128)S(1)}) custom-call(s32[1,24]{1,0:T(1,128)S(1)} %pad_add_fusion.1.meta.places, f32[2,2,256,256]{3,2,1,0:T(8,128)S(1)} %copy-done, f32[8,256,256]{2,1,0:T(8,128)} %arrange.1.amplitudes, f32[2,512,512]{2,1,0:T(8,128)} %tile.13, ...), custom_call_target="tpu_custom_call" | custom-call | flops 12000000000 | bytes 16000000 | tf_op jit(solution)/shard_map/slots_inside/pallas_call | solution.py:544
  32.1 1.0 copy-done.4
  33.1 3.5 %slots_beyond.1 = (f32[2,768,768]{2,1,0:T(8,128)S(1)}, f32[2,768,768]{2,1,0:T(8,128)S(1)}, f32[5,256,256]{2,1,0:T(8,128)S(1)}, f32[2,512,512]{2,1,0:T(8,128)}, f...) custom-call(s32[1,24]{1,0:T(1,128)S(1)} %pad_add_fusion.1.meta.place, ...), custom_call_target="tpu_custom_call", output_to_operand_aliasing={{0}: (9, {}), {1}: (10, {}), {2}: (11, {})} | custom-call | flops 12000000000 | bytes 16000000 | tf_op jit(solution)/shard_map/slots_beyond/pallas_call | solution.py:576
  36.7 6.4 %collective-permute-start.4 = (f32[5,128,256]{2,1,0:T(8,128)S(1)}, f32[5,128,256]{2,1,0:T(8,128)S(1)}, u32[]{:S(2)}, u32[]{:S(2)}) collective-permute-start(f32[5,128,256]{2,1,0:T(8,128)S(1)} %get-tuple-element.69), channel_id=1, source_target_pairs={{0,8},{8,0},{16,24},{24,16},{1,9},{9,1},{17,25},{25,17},{2,10},{10... | collective-permute-start | bytes 1966088 | tf_op jit(solution)/shard_map/ppermute | solution.py:711
  43.1 1.7 %collective-permute-done.4.got = f32[5,128,256]{2,1,0:T(8,128)S(1)} collective-permute-done((f32[5,128,256]{2,1,0:T(8,128)S(1)}, f32[5,128,256]{2,1,0:T(8,128)S(1)}, u32[]{:S(2)}, u32[]{:S(2)}) %collective-permute-start.4) | collective-permute-done | bytes 655392 | tf_op jit(solution)/shard_map/ppermute | solution.py:711
  45.5 10.0 %collective-permute-done.5.refs_1_ = f32[5,64,256]{2,1,0:T(8,128)S(1)} collective-permute-done((f32[5,64,256]{2,1,0:T(8,128)S(1)}, f32[5,64,256]{2,1,0:T(8,128)S(1)}, u32[]{:S(2)}, u32[]{:S(2)}) %collective-permute-start.5) | collective-permute-done | bytes 327712 | tf_op jit(solution)/shard_map/ppermute | solution.py:711
  56.3 17.8 %all-to-all-start = ((f32[8,5,8,256]{3,2,1,0:T(8,128)}), f32[8,5,8,256]{3,2,1,0:T(8,128)S(1)}, u32[]{:S(2)}, u32[]{:S(2)}) async-start(f32[8,5,8,256]{3,2,1,0:T(8,128)} %deal.1), calls=%async_computation | async-start | bytes 655360 | tf_op jit(solution)/shard_map/all_to_all | solution.py:962
  74.1 4.1 %collective-permute-start.6 = (f32[2,264,256]{2,1,0:T(8,128)S(1)}, f32[2,264,256]{2,1,0:T(8,128)S(1)}, u32[]{:S(2)}, u32[]{:S(2)}) collective-permute-start(f32[2,264,256]{2,1,0:T(8,128)S(1)} %get-tuple-element.72), channel_id=1, source_target_pairs={{0,1},{1,2},{2,3},{3,4},{4,5},{5,6},{6,7},{8,9},{9,10},{10,11},{11... | collective-permute-start | bytes 1622024 | tf_op jit(solution)/shard_map/ppermute | solution.py:706
  78.1 6.1 %all-to-all-done.pieces = f32[8,5,8,256]{3,2,1,0:T(8,128)S(1)} async-done(((f32[8,5,8,256]{3,2,1,0:T(8,128)}), f32[8,5,8,256]{3,2,1,0:T(8,128)S(1)}, u32[]{:S(2)}, u32[]{:S(2)}) %all-to-all-start) | async-done | bytes 327712 | tf_op jit(solution)/shard_map/all_to_all | solution.py:962
  84.2 2.0 %settle.1 = f32[8,4,8,256]{3,2,1,0:T(8,128)} custom-call(s32[1,24]{1,0:T(1,128)S(1)} %pad_add_fusion.1.meta.places, f32[4,256,256]{2,1,0:T(8,128)} %bitcast.13, f32[8,5,8,256]{3,2,1,0:T(8,128)S(1)} %all-to-all-done.pieces), custom_call_target="tpu_custom_call" | custom-call | bytes 1000000 | tf_op jit(solution)/shard_map/settle/pallas_call | solution.py:852
  86.2 4.5 %collective-permute-done.6.bottom = f32[2,264,256]{2,1,0:T(8,128)S(1)} collective-permute-done((f32[2,264,256]{2,1,0:T(8,128)S(1)}, f32[2,264,256]{2,1,0:T(8,128)S(1)}, u32[]{:S(2)}, u32[]{:S(2)}) %collective-permute-start.6) | collective-permute-done | bytes 540704 | tf_op jit(solution)/shard_map/ppermute | solution.py:706
  90.7 1.3 %collective-permute-start.7 = (f32[2,264,256]{2,1,0:T(8,128)}, f32[2,264,256]{2,1,0:T(8,128)S(1)}, u32[]{:S(2)}, u32[]{:S(2)}) collective-permute-start(f32[2,264,256]{2,1,0:T(8,128)} %get-tuple-element.76), channel_id=1, source_target_pairs={{0,8},{8,16},{16,24},{1,9},{9,17},{17,25},{2,10},{10,18},{18,26},{... | collective-permute-start | bytes 1622024 | tf_op jit(solution)/shard_map/ppermute | solution.py:706
  92.0 7.7 %all-to-all-start.1 = ((f32[8,4,8,256]{3,2,1,0:T(8,128)}), f32[8,4,8,256]{3,2,1,0:T(8,128)S(1)}, u32[]{:S(2)}, u32[]{:S(2)}) async-start(f32[8,4,8,256]{3,2,1,0:T(8,128)} %settle.1), calls=%async_computation.1 | async-start | bytes 524288 | tf_op jit(solution)/shard_map/all_to_all | solution.py:967
  99.8 3.8 %collective-permute-start.9 = (f32[2,264,512]{2,1,0:T(8,128)S(1)}, f32[2,264,512]{2,1,0:T(8,128)S(1)}, u32[]{:S(2)}, u32[]{:S(2)}) collective-permute-start(f32[2,264,512]{2,1,0:T(8,128)S(1)} %annotate.1), channel_id=1, source_target_pairs={{0,8},{8,16},{16,24},{1,9},{9,17},{17,25},{2,10},{10,18},{18,26},{... | collective-permute-start | bytes 3244040 | tf_op jit(solution)/shard_map/ppermute | solution.py:706
  103.6 5.3 %all-to-all-done.1.pieces = f32[8,4,8,256]{3,2,1,0:T(8,128)S(1)} async-done(((f32[8,4,8,256]{3,2,1,0:T(8,128)}), f32[8,4,8,256]{3,2,1,0:T(8,128)S(1)}, u32[]{:S(2)}, u32[]{:S(2)}) %all-to-all-start.1) | async-done | bytes 262176 | tf_op jit(solution)/shard_map/all_to_all | solution.py:967
  109.0 1.0 copy-done.2
  110.1 1.1 collective-permute-start.8
  111.2 2.1 %collective-permute-start.11 = (f32[2,256,256]{2,1,0:T(8,128)S(1)}, f32[2,256,256]{2,1,0:T(8,128)S(1)}, u32[]{:S(2)}, u32[]{:S(2)}) collective-permute-start(f32[2,256,256]{2,1,0:T(8,128)S(1)} %merge.1), channel_id=1, source_target_pairs={{0,1},{1,2},{2,3},{3,4},{4,5},{5,6},{6,7},{8,9},{9,10},{10,11},{11... | collective-permute-start | bytes 1572872 | tf_op jit(solution)/shard_map/ppermute | solution.py:706
  113.3 2.7 %light.1.scale = f32[512,512]{1,0:T(8,128)S(1)} custom-call(s32[1,24]{1,0:T(1,128)S(1)} %pad_add_fusion.1.meta.places, f32[2,2,256,256]{3,2,1,0:T(8,128)} %probe_h.1, f32[2,264,256]{2,1,0:T(8,128)S(1)} %collective-permute-done.6.bottom, f32[2,264,256]{2,1,0:T(8,128)S(1)} %collective-permute-done.7.corner, f32[2,264,512]{2,1,0:T(8,128)S(1)} %collective-permute-done.9.lower), custom_call_target="tpu_custom_call" | custom-call | flops 4000000000 | bytes 4000000 | tf_op jit(solution)/shard_map/light/pallas_call | solution.py:177
  116.1 3.2 %collective-permute-done.8.other = f32[4,64,256]{2,1,0:T(8,128)S(1)} collective-permute-done((f32[4,64,256]{2,1,0:T(8,128)S(1)}, f32[4,64,256]{2,1,0:T(8,128)S(1)}, u32[]{:S(2)}, u32[]{:S(2)}) %collective-permute-start.8) | collective-permute-done | bytes 262176 | tf_op jit(solution)/shard_map/ppermute | solution.py:711
  120.0 2.5 %collective-permute-start.10 = (f32[4,128,256]{2,1,0:T(8,128)S(1)}, f32[4,128,256]{2,1,0:T(8,128)S(1)}, u32[]{:S(2)}, u32[]{:S(2)}) collective-permute-start(f32[4,128,256]{2,1,0:T(8,128)S(1)} %join.2.mine), channel_id=1, source_target_pairs={{0,8},{8,0},{16,24},{24,16},{1,9},{9,1},{17,25},{25,17},{2,10},{10... | collective-permute-start | bytes 1572872 | tf_op jit(solution)/shard_map/ppermute | solution.py:711
  122.4 3.2 %finish_far.1.before = f32[2,512,512]{2,1,0:T(8,128)} custom-call(f32[2,512,512]{2,1,0:T(8,128)} %get-tuple-element.85.own, f32[2,264,256]{2,1,0:T(8,128)S(1)} %collective-permute-done.6.bottom, f32[2,264,512]{2,1,0:T(8,128)S(1)} %collective-permute-done.9.lower, f32[512,512]{1,0:T(8,128)S(1)} %light.1.scale, f32[2,512,512]{2,1,0:T(8,128)} %tile.13), custom_call_target="tpu_custom_call" | custom-call | flops 2000000000 | bytes 4000000 | tf_op jit(solution)/shard_map/finish_far/pallas_call | solution.py:640
  125.7 1.9 %finish_near.1 = f32[2,512,512]{2,1,0:T(8,128)} custom-call(f32[2,512,512]{2,1,0:T(8,128)} %finish_far.1.before, f32[2,256,256]{2,1,0:T(8,128)S(1)} %collective-permute-done.11.top, f32[512,512]{1,0:T(8,128)S(1)} %light.1.scale), custom_call_target="tpu_custom_call", output_to_operand_aliasing={{}: (0, {})} | custom-call | flops 2000000000 | bytes 4000000 | tf_op jit(solution)/shard_map/finish_near/pallas_call | solution.py:684
  127.6 1.5 %join.3 = f32[4,256,256]{2,1,0:T(8,128)} custom-call(s32[1,24]{1,0:T(1,128)S(1)} %pad_add_fusion.1.meta.places, f32[4,128,256]{2,1,0:T(8,128)S(1)} %join.2.mine, f32[4,128,256]{2,1,0:T(8,128)S(1)} %collective-permute-done.10.other), custom_call_target="tpu_custom_call" | custom-call | bytes 2000000 | tf_op jit(solution)/shard_map/join/pallas_call | solution.py:900
  (34 shorter events, 3.6 us)
Async XLA Ops:
  2.8 6.0 %copy-start.5 = (s32[8,2]{0,1:T(2,128)S(1)}, s32[8,2]{0,1:T(2,128)}, u32[]{:S(2)}) copy-start(s32[8,2]{0,1:T(2,128)} %param.12) | copy-start | bytes 196
  2.9 17.8 %collective-permute-start = (f32[2,256,256]{2,1,0:T(8,128)}, f32[2,256,256]{2,1,0:T(8,128)S(1)}, u32[]{:S(2)}, u32[]{:S(2)}) collective-permute-start(f32[2,256,256]{2,1,0:T(8,128)} %get-tuple-element.50), channel_id=1, source_target_pairs={{1,0},{2,1},{3,2},{4,3},{5,4},{6,5},{7,6},{9,8},{10,9},{11,10},{12... | collective-permute-start | bytes 1572872 | tf_op jit(solution)/shard_map/ppermute | solution.py:706
  4.2 27.1 %collective-permute-start.2 = (f32[2,256,256]{2,1,0:T(8,128)}, f32[2,256,256]{2,1,0:T(8,128)S(1)}, u32[]{:S(2)}, u32[]{:S(2)}) collective-permute-start(f32[2,256,256]{2,1,0:T(8,128)} %get-tuple-element.55), channel_id=1, source_target_pairs={{1,0},{2,1},{3,2},{4,3},{5,4},{6,5},{7,6},{9,8},{10,9},{11,10},{12... | collective-permute-start | bytes 1572872 | tf_op jit(solution)/shard_map/ppermute | solution.py:706
  6.7 15.3 %collective-permute-start.1 = (f32[2,256,512]{2,1,0:T(8,128)S(1)}, f32[2,256,512]{2,1,0:T(8,128)S(1)}, u32[]{:S(2)}, u32[]{:S(2)}) collective-permute-start(f32[2,256,512]{2,1,0:T(8,128)S(1)} %cut_lower.1), channel_id=1, source_target_pairs={{8,0},{16,8},{24,16},{9,1},{17,9},{25,17},{10,2},{18,10},{26,18},{... | collective-permute-start | bytes 3145736 | tf_op jit(solution)/shard_map/ppermute | solution.py:706
  9.2 12.7 %copy-start = (f32[2,2,256,256]{3,2,1,0:T(8,128)S(1)}, f32[2,2,256,256]{3,2,1,0:T(8,128)}, u32[]{:S(2)}) copy-start(f32[2,2,256,256]{3,2,1,0:T(8,128)} %probe_h.1) | copy-start | bytes 3145732
  20.7 11.4 %collective-permute-start.3 = (f32[2,256,256]{2,1,0:T(8,128)S(1)}, f32[2,256,256]{2,1,0:T(8,128)S(1)}, u32[]{:S(2)}, u32[]{:S(2)}) collective-permute-start(f32[2,256,256]{2,1,0:T(8,128)S(1)} %collective-permute-done.refs_0_), channel_id=1, source_target_pairs={{8,0},{16,8},{24,16},{9,1},{17,9},{25,17},{10,2},{18,10},{26,18},{... | collective-permute-start | bytes 1572872 | tf_op jit(solution)/shard_map/ppermute | solution.py:706
  31.3 0.8 copy-start.3
  32.1 1.0 copy-start.4
  36.7 8.8 %copy-start.1 = (f32[2,256,256]{2,1,0:T(8,128)}, f32[2,256,256]{2,1,0:T(8,128)S(1)}, u32[]{:S(2)}) copy-start(f32[2,256,256]{2,1,0:T(8,128)S(1)} %get-tuple-element.67.top) | copy-start | bytes 1572868
  36.7 8.1 %collective-permute-start.4 = (f32[5,128,256]{2,1,0:T(8,128)S(1)}, f32[5,128,256]{2,1,0:T(8,128)S(1)}, u32[]{:S(2)}, u32[]{:S(2)}) collective-permute-start(f32[5,128,256]{2,1,0:T(8,128)S(1)} %get-tuple-element.69), channel_id=1, source_target_pairs={{0,8},{8,0},{16,24},{24,16},{1,9},{9,1},{17,25},{25,17},{2,10},{10... | collective-permute-start | bytes 1966088 | tf_op jit(solution)/shard_map/ppermute | solution.py:711
  45.4 10.1 %collective-permute-start.5 = (f32[5,64,256]{2,1,0:T(8,128)S(1)}, f32[5,64,256]{2,1,0:T(8,128)S(1)}, u32[]{:S(2)}, u32[]{:S(2)}) collective-permute-start(f32[5,64,256]{2,1,0:T(8,128)S(1)} %get-tuple-element.71), channel_id=1, source_target_pairs={{0,16},{8,24},{16,0},{24,8},{1,17},{9,25},{17,1},{25,9},{2,18},{10... | collective-permute-start | bytes 983048 | tf_op jit(solution)/shard_map/ppermute | solution.py:711
  56.3 27.9 %all-to-all-start = ((f32[8,5,8,256]{3,2,1,0:T(8,128)}), f32[8,5,8,256]{3,2,1,0:T(8,128)S(1)}, u32[]{:S(2)}, u32[]{:S(2)}) async-start(f32[8,5,8,256]{3,2,1,0:T(8,128)} %deal.1), calls=%async_computation | async-start | bytes 655360 | tf_op jit(solution)/shard_map/all_to_all | solution.py:962
  74.1 16.7 %collective-permute-start.6 = (f32[2,264,256]{2,1,0:T(8,128)S(1)}, f32[2,264,256]{2,1,0:T(8,128)S(1)}, u32[]{:S(2)}, u32[]{:S(2)}) collective-permute-start(f32[2,264,256]{2,1,0:T(8,128)S(1)} %get-tuple-element.72), channel_id=1, source_target_pairs={{0,1},{1,2},{2,3},{3,4},{4,5},{5,6},{6,7},{8,9},{9,10},{10,11},{11... | collective-permute-start | bytes 1622024 | tf_op jit(solution)/shard_map/ppermute | solution.py:706
  90.7 18.2 %collective-permute-start.7 = (f32[2,264,256]{2,1,0:T(8,128)}, f32[2,264,256]{2,1,0:T(8,128)S(1)}, u32[]{:S(2)}, u32[]{:S(2)}) collective-permute-start(f32[2,264,256]{2,1,0:T(8,128)} %get-tuple-element.76), channel_id=1, source_target_pairs={{0,8},{8,16},{16,24},{1,9},{9,17},{17,25},{2,10},{10,18},{18,26},{... | collective-permute-start | bytes 1622024 | tf_op jit(solution)/shard_map/ppermute | solution.py:706
  92.0 16.9 %all-to-all-start.1 = ((f32[8,4,8,256]{3,2,1,0:T(8,128)}), f32[8,4,8,256]{3,2,1,0:T(8,128)S(1)}, u32[]{:S(2)}, u32[]{:S(2)}) async-start(f32[8,4,8,256]{3,2,1,0:T(8,128)} %settle.1), calls=%async_computation.1 | async-start | bytes 524288 | tf_op jit(solution)/shard_map/all_to_all | solution.py:967
  99.8 13.5 %collective-permute-start.9 = (f32[2,264,512]{2,1,0:T(8,128)S(1)}, f32[2,264,512]{2,1,0:T(8,128)S(1)}, u32[]{:S(2)}, u32[]{:S(2)}) collective-permute-start(f32[2,264,512]{2,1,0:T(8,128)S(1)} %annotate.1), channel_id=1, source_target_pairs={{0,8},{8,16},{16,24},{1,9},{9,17},{17,25},{2,10},{10,18},{18,26},{... | collective-permute-start | bytes 3244040 | tf_op jit(solution)/shard_map/ppermute | solution.py:706
  109.0 1.0 copy-start.2
  110.1 9.2 %collective-permute-start.8 = (f32[4,64,256]{2,1,0:T(8,128)S(1)}, f32[4,64,256]{2,1,0:T(8,128)S(1)}, u32[]{:S(2)}, u32[]{:S(2)}) collective-permute-start(f32[4,64,256]{2,1,0:T(8,128)S(1)} %collect.1.mine), channel_id=1, source_target_pairs={{0,16},{8,24},{16,0},{24,8},{1,17},{9,25},{17,1},{25,9},{2,18},{10... | collective-permute-start | bytes 786440 | tf_op jit(solution)/shard_map/ppermute | solution.py:711
  111.2 14.5 %collective-permute-start.11 = (f32[2,256,256]{2,1,0:T(8,128)S(1)}, f32[2,256,256]{2,1,0:T(8,128)S(1)}, u32[]{:S(2)}, u32[]{:S(2)}) collective-permute-start(f32[2,256,256]{2,1,0:T(8,128)S(1)} %merge.1), channel_id=1, source_target_pairs={{0,1},{1,2},{2,3},{3,4},{4,5},{5,6},{6,7},{8,9},{9,10},{10,11},{11... | collective-permute-start | bytes 1572872 | tf_op jit(solution)/shard_map/ppermute | solution.py:706
  120.0 7.7 %collective-permute-start.10 = (f32[4,128,256]{2,1,0:T(8,128)S(1)}, f32[4,128,256]{2,1,0:T(8,128)S(1)}, u32[]{:S(2)}, u32[]{:S(2)}) collective-permute-start(f32[4,128,256]{2,1,0:T(8,128)S(1)} %join.2.mine), channel_id=1, source_target_pairs={{0,8},{8,0},{16,24},{24,16},{1,9},{9,1},{17,25},{25,17},{2,10},{10... | collective-permute-start | bytes 1572872 | tf_op jit(solution)/shard_map/ppermute | solution.py:711

commit v2 on v1

--- a/solution.py
+++ b/solution.py
@@ -959,19 +959,20 @@
         if k + 1 < len(bits):
             send, share = fold(mine, index, share, got, bit_at + k + 1)
             index = None
+    got, bottom_spill, lower_spill = together(got, bottom_spill, lower_spill)
+    lower_spill = from_behind(annotate(lower_spill, bottom_spill), "row", 1)
     pieces = lax.all_to_all(deal([share, got], parts, rows), "col", 0, 0, tiled=True)
     new = settle(mine, start_at, probe.reshape(2 * modes, size, size), pieces)
-    new, bottom_spill, lower_spill, corner_spill = together(new, bottom_spill, lower_spill, corner_spill)
+    new, lower_spill, corner_spill = together(new, lower_spill, corner_spill)
     corner_spill = from_behind(corner_spill, "row", 1)
-    lower_spill = from_behind(annotate(lower_spill, bottom_spill), "row", 1)
+    inverse_light = light(
+        mine, slots, origin_at, probe, bottom_spill, corner_spill, lower_spill, (tile_rows, tile_cols)
+    )
     new = lax.all_to_all(new, "col", 0, 0, tiled=True)
     new, corner_spill = together(new, corner_spill)
     top_spill, new = together(merge(top_spill, corner_spill), new)
     top_spill = from_behind(top_spill, "col", 1)
     new = collect(new)
-    inverse_light = light(
-        mine, slots, origin_at, probe, bottom_spill, corner_spill, lower_spill, (tile_rows, tile_cols)
-    )
     for k, bit in reversed(list(enumerate(bits))):
         if k == 0:
             new, own = together(new, own)

time: 131 us -> 123 us (0.939)
  blocking collectives: 0 us -> 33.9 us
  starting transfers between devices: 52.1 us -> 29.3 us
  waiting for transfers between devices: 39.2 us -> 21.4 us
  local copies, waits for them, and re-layouts: 3.23 us -> 0.35 us
  Pallas kernels: 32.8 us -> 35.6 us
    all_to_all x0 -> x2, blocking collectives: none -> 33.9 us  [the longest x1 22 us: body(): lax.all_to_all(deal([share, got], parts, rows), 'col', 0, 0, tiled=True)]
    all_to_all x2 -> x0, starting transfers between devices: 25.6 us -> none  [the longest x1 17.8 us: body(): lax.all_to_all(deal([share, got], parts, rows), 'col', 0, 0, tiled=True)]
    all_to_all x2 -> x0, waiting for transfers between devices: 11.4 us -> none  [the longest x1 6.05 us: body(): lax.all_to_all(deal([share, got], parts, rows), 'col', 0, 0, tiled=True)]
    ppermute x4, waiting for transfers between devices: 14.9 us -> 6.19 us  [exchange(): return lax.ppermute(array, axis, [(i, i ^ bit) for i in range(count)])]
    pallas_call x1, Pallas kernels: 3.52 us -> 7.13 us  [visit_beyond(): pl.pallas_call(kernel, out_shape=[pltpu.VMEM(item.shape, item.dtype) for...]
    unnamed x13 -> x5, local copies, waits for them, and re-layouts: 2.97 us -> 0.09 us
    ppermute x4, starting transfers between devices: 10.1 us -> 12.7 us  [exchange(): return lax.ppermute(array, axis, [(i, i ^ bit) for i in range(count)])]
    ppermute x8, waiting for transfers between devices: 12.9 us -> 15.2 us  [from_behind(): return lax.ppermute(array, axis, pairs)]
  transfers between devices with their start and end apart: 14 -> 12, of which waited for: 7 -> 6; matrix products, arithmetic and copies ran while one was open for 0% -> 0% of each run, Pallas kernels for 19% -> 20%
where the time goes in v2:
time: 123 us; the launch traced here: 122 us
  Pallas kernels  35.6 us (29%)
  blocking collectives  33.9 us (28%)
  starting transfers between devices  29.3 us (24%)
  waiting for transfers between devices  21.4 us (17%)
  between operations  1.68 us (1%)
    all_to_all x1, blocking collectives, body(): lax.all_to_all(deal([share, got], parts, rows), 'col', 0, 0, tiled=True)  22 us
    ppermute x8, starting transfers between devices, from_behind(): return lax.ppermute(array, axis, pairs)  16.6 us
    ppermute x8, waiting for transfers between devices, from_behind(): return lax.ppermute(array, axis, pairs)  15.2 us
    ppermute x4, starting transfers between devices, exchange(): return lax.ppermute(array, axis, [(i, i ^ bit) for i in range(count)])  12.7 us
    all_to_all x1, blocking collectives, body(): new = lax.all_to_all(new, 'col', 0, 0, tiled=True)  11.8 us
    pallas_call x1, Pallas kernels, visit_inside(): pl.pallas_call(kernel, out_shape=[field, field, pltpu.VMEM((2 * modes + 1...  9.25 us
    pallas_call x1, Pallas kernels, visit_beyond(): pl.pallas_call(kernel, out_shape=[pltpu.VMEM(item.shape, item.dtype) for...  7.13 us
    ppermute x4, waiting for transfers between devices, exchange(): return lax.ppermute(array, axis, [(i, i ^ bit) for i in range(count)])  6.19 us
  transfers between devices with their start and end apart: 12, of which 6 were waited for; matrix products, arithmetic and copies ran while one was open for 0% of the time, Pallas kernels for 20%

profile of v2, /device:TPU:0, one launch (start us, length us, event | category | flops | bytes accessed | tf_op | source)
XLA Modules:
  0.0 122.5 jit_solution(2787094777261979886)
XLA Ops:
  0.6 2.2 %cut_right.1 = (f32[2,256,256]{2,1,0:T(8,128)}, f32[2,256,256]{2,1,0:T(8,128)}) custom-call(f32[2,512,512]{2,1,0:T(8,128)} %tile.13), custom_call_target="tpu_custom_call" | custom-call | bytes 1000000 | tf_op jit(solution)/shard_map/cut_right/pallas_call | solution.py:730
  2.8 1.3 %collective-permute-start = (f32[2,256,256]{2,1,0:T(8,128)}, f32[2,256,256]{2,1,0:T(8,128)S(1)}, u32[]{:S(2)}, u32[]{:S(2)}) collective-permute-start(f32[2,256,256]{2,1,0:T(8,128)} %get-tuple-element.52), channel_id=1, source_target_pairs={{1,0},{2,1},{3,2},{4,3},{5,4},{6,5},{7,6},{9,8},{10,9},{11,10},{12... | collective-permute-start | bytes 1572872 | tf_op jit(solution)/shard_map/ppermute | solution.py:706
  4.1 1.3 %collective-permute-start.2 = (f32[2,256,256]{2,1,0:T(8,128)}, f32[2,256,256]{2,1,0:T(8,128)S(1)}, u32[]{:S(2)}, u32[]{:S(2)}) collective-permute-start(f32[2,256,256]{2,1,0:T(8,128)} %get-tuple-element.57), channel_id=1, source_target_pairs={{1,0},{2,1},{3,2},{4,3},{5,4},{6,5},{7,6},{9,8},{10,9},{11,10},{12... | collective-permute-start | bytes 1572872 | tf_op jit(solution)/shard_map/ppermute | solution.py:706
  5.4 1.2 %cut_lower.1 = f32[2,256,512]{2,1,0:T(8,128)S(1)} custom-call(f32[2,512,512]{2,1,0:T(8,128)} %tile.13), custom_call_target="tpu_custom_call" | custom-call | flops 30000001024 | bytes 4000000 | tf_op jit(solution)/shard_map/cut_lower/pallas_call | solution.py:730
  6.7 1.3 %collective-permute-start.1 = (f32[2,256,512]{2,1,0:T(8,128)S(1)}, f32[2,256,512]{2,1,0:T(8,128)S(1)}, u32[]{:S(2)}, u32[]{:S(2)}) collective-permute-start(f32[2,256,512]{2,1,0:T(8,128)S(1)} %cut_lower.1), channel_id=1, source_target_pairs={{8,0},{16,8},{24,16},{9,1},{17,9},{25,17},{10,2},{18,10},{26,18},{... | collective-permute-start | bytes 3145736 | tf_op jit(solution)/shard_map/ppermute | solution.py:706
  9.2 3.5 %arrange.1.amplitudes = f32[8,256,256]{2,1,0:T(8,128)} custom-call(s32[1,24]{1,0:T(1,128)S(1)} %pad_add_fusion.1.meta.places, f32[8,256,256]{2,1,0:T(8,128)} %amplitudes.1), custom_call_target="tpu_custom_call" | custom-call | flops 30000001024 | bytes 4000000 | tf_op jit(solution)/shard_map/arrange/pallas_call | solution.py:244
  12.7 8.0 %collective-permute-done.refs_0_ = f32[2,256,256]{2,1,0:T(8,128)S(1)} collective-permute-done((f32[2,256,256]{2,1,0:T(8,128)}, f32[2,256,256]{2,1,0:T(8,128)S(1)}, u32[]{:S(2)}, u32[]{:S(2)}) %collective-permute-start) | collective-permute-done | bytes 524320 | tf_op jit(solution)/shard_map/ppermute | solution.py:706
  20.7 1.3 %collective-permute-start.3 = (f32[2,256,256]{2,1,0:T(8,128)S(1)}, f32[2,256,256]{2,1,0:T(8,128)S(1)}, u32[]{:S(2)}, u32[]{:S(2)}) collective-permute-start(f32[2,256,256]{2,1,0:T(8,128)S(1)} %collective-permute-done.refs_0_), channel_id=1, source_target_pairs={{8,0},{16,8},{24,16},{9,1},{17,9},{25,17},{10,2},{18,10},{26,18},{... | collective-permute-start | bytes 1572872 | tf_op jit(solution)/shard_map/ppermute | solution.py:706
  22.0 9.3 %slots_inside.1 = (f32[2,768,768]{2,1,0:T(8,128)S(1)}, f32[2,768,768]{2,1,0:T(8,128)S(1)}, f32[5,256,256]{2,1,0:T(8,128)S(1)}) custom-call(s32[1,24]{1,0:T(1,128)S(1)} %pad_add_fusion.1.meta.places, f32[2,2,256,256]{3,2,1,0:T(8,128)S(1)} %copy-done, f32[8,256,256]{2,1,0:T(8,128)} %arrange.1.amplitudes, f32[2,512,512]{2,1,0:T(8,128)} %tile.13, ...), custom_call_target="tpu_custom_call" | custom-call | flops 12000000000 | bytes 16000000 | tf_op jit(solution)/shard_map/slots_inside/pallas_call | solution.py:544
  31.3 7.1 %slots_beyond.1 = (f32[2,768,768]{2,1,0:T(8,128)S(1)}, f32[2,768,768]{2,1,0:T(8,128)S(1)}, f32[5,256,256]{2,1,0:T(8,128)S(1)}, f32[2,512,512]{2,1,0:T(8,128)}, f...) custom-call(s32[1,24]{1,0:T(1,128)S(1)} %pad_add_fusion.1.meta.place, ...), custom_call_target="tpu_custom_call", output_to_operand_aliasing={{0}: (9, {}), {1}: (10, {}), {2}: (11, {})} | custom-call | flops 12000000000 | bytes 16000000 | tf_op jit(solution)/shard_map/slots_beyond/pallas_call | solution.py:576
  38.4 3.5 %collective-permute-start.4 = (f32[5,128,256]{2,1,0:T(8,128)S(1)}, f32[5,128,256]{2,1,0:T(8,128)S(1)}, u32[]{:S(2)}, u32[]{:S(2)}) collective-permute-start(f32[5,128,256]{2,1,0:T(8,128)S(1)} %get-tuple-element.71), channel_id=1, source_target_pairs={{0,8},{8,0},{16,24},{24,16},{1,9},{9,1},{17,25},{25,17},{2,10},{10... | collective-permute-start | bytes 1966088 | tf_op jit(solution)/shard_map/ppermute | solution.py:711
  41.9 1.5 %collective-permute-start.6 = (f32[2,264,256]{2,1,0:T(8,128)S(1)}, f32[2,264,256]{2,1,0:T(8,128)S(1)}, u32[]{:S(2)}, u32[]{:S(2)}) collective-permute-start(f32[2,264,256]{2,1,0:T(8,128)S(1)} %get-tuple-element.74), channel_id=1, source_target_pairs={{0,1},{1,2},{2,3},{3,4},{4,5},{5,6},{6,7},{8,9},{9,10},{10,11},{11... | collective-permute-start | bytes 1622024 | tf_op jit(solution)/shard_map/ppermute | solution.py:706
  43.4 0.2 collective-permute-done.4.got
  43.6 0.6 fold.1
  44.2 7.1 %collective-permute-start.5 = (f32[5,64,256]{2,1,0:T(8,128)S(1)}, f32[5,64,256]{2,1,0:T(8,128)S(1)}, u32[]{:S(2)}, u32[]{:S(2)}) collective-permute-start(f32[5,64,256]{2,1,0:T(8,128)S(1)} %get-tuple-element.73), channel_id=1, source_target_pairs={{0,16},{8,24},{16,0},{24,8},{1,17},{9,25},{17,1},{25,9},{2,18},{10... | collective-permute-start | bytes 983048 | tf_op jit(solution)/shard_map/ppermute | solution.py:711
  51.3 4.2 %collective-permute-done.6.bottom = f32[2,264,256]{2,1,0:T(8,128)S(1)} collective-permute-done((f32[2,264,256]{2,1,0:T(8,128)S(1)}, f32[2,264,256]{2,1,0:T(8,128)S(1)}, u32[]{:S(2)}, u32[]{:S(2)}) %collective-permute-start.6) | collective-permute-done | bytes 540704 | tf_op jit(solution)/shard_map/ppermute | solution.py:706
  55.5 3.9 %collective-permute-done.5.refs_1_ = f32[5,64,256]{2,1,0:T(8,128)S(1)} collective-permute-done((f32[5,64,256]{2,1,0:T(8,128)S(1)}, f32[5,64,256]{2,1,0:T(8,128)S(1)}, u32[]{:S(2)}, u32[]{:S(2)}) %collective-permute-start.5) | collective-permute-done | bytes 327712 | tf_op jit(solution)/shard_map/ppermute | solution.py:711
  59.4 1.7 %collective-permute-start.7 = (f32[2,264,512]{2,1,0:T(8,128)S(1)}, f32[2,264,512]{2,1,0:T(8,128)S(1)}, u32[]{:S(2)}, u32[]{:S(2)}) collective-permute-start(f32[2,264,512]{2,1,0:T(8,128)S(1)} %annotate.1), channel_id=1, source_target_pairs={{0,8},{8,16},{16,24},{1,9},{9,17},{17,25},{2,10},{10,18},{18,26},{... | collective-permute-start | bytes 3244040 | tf_op jit(solution)/shard_map/ppermute | solution.py:706
  61.1 22.0 %all_to_all.10.pieces = f32[8,5,8,256]{3,2,1,0:T(8,128)S(1)} all-to-all(f32[8,5,8,256]{3,2,1,0:T(8,128)S(1)} %deal.1), channel_id=1, replica_groups=mesh['row'=4,'col'=8] {'col'}, dimensions={0} | all-to-all | bytes 655360 | tf_op jit(solution)/shard_map/all_to_all | solution.py:964
  83.2 1.3 %settle.1 = f32[8,4,8,256]{3,2,1,0:T(8,128)S(1)} custom-call(s32[1,24]{1,0:T(1,128)S(1)} %pad_add_fusion.1.meta.places, f32[4,256,256]{2,1,0:T(8,128)} %bitcast.13, f32[8,5,8,256]{3,2,1,0:T(8,128)S(1)} %all_to_all.10.pieces), custom_call_target="tpu_custom_call" | custom-call | bytes 1000000 | tf_op jit(solution)/shard_map/settle/pallas_call | solution.py:852
  84.5 6.3 %collective-permute-start.8 = (f32[2,264,256]{2,1,0:T(8,128)S(1)}, f32[2,264,256]{2,1,0:T(8,128)S(1)}, u32[]{:S(2)}, u32[]{:S(2)}) collective-permute-start(f32[2,264,256]{2,1,0:T(8,128)S(1)} %get-tuple-element.81), channel_id=1, source_target_pairs={{0,8},{8,16},{16,24},{1,9},{9,17},{17,25},{2,10},{10,18},{18,26},{... | collective-permute-start | bytes 1622024 | tf_op jit(solution)/shard_map/ppermute | solution.py:706
  90.9 11.8 %all_to_all.11.pieces = f32[8,4,8,256]{3,2,1,0:T(8,128)S(1)} all-to-all(f32[8,4,8,256]{3,2,1,0:T(8,128)S(1)} %settle.1), channel_id=1, replica_groups=mesh['row'=4,'col'=8] {'col'}, dimensions={0} | all-to-all | bytes 524288 | tf_op jit(solution)/shard_map/all_to_all | solution.py:971
  102.8 1.9 %collective-permute-start.9 = (f32[4,64,256]{2,1,0:T(8,128)S(1)}, f32[4,64,256]{2,1,0:T(8,128)S(1)}, u32[]{:S(2)}, u32[]{:S(2)}) collective-permute-start(f32[4,64,256]{2,1,0:T(8,128)S(1)} %collect.1.mine), channel_id=1, source_target_pairs={{0,16},{8,24},{16,0},{24,8},{1,17},{9,25},{17,1},{25,9},{2,18},{10... | collective-permute-start | bytes 786440 | tf_op jit(solution)/shard_map/ppermute | solution.py:711
  104.7 1.9 %collective-permute-start.11 = (f32[2,256,256]{2,1,0:T(8,128)S(1)}, f32[2,256,256]{2,1,0:T(8,128)S(1)}, u32[]{:S(2)}, u32[]{:S(2)}) collective-permute-start(f32[2,256,256]{2,1,0:T(8,128)S(1)} %merge.1), channel_id=1, source_target_pairs={{0,1},{1,2},{2,3},{3,4},{4,5},{5,6},{6,7},{8,9},{9,10},{10,11},{11... | collective-permute-start | bytes 1572872 | tf_op jit(solution)/shard_map/ppermute | solution.py:706
  106.6 3.0 %light.1.scale = f32[512,512]{1,0:T(8,128)S(1)} custom-call(s32[1,24]{1,0:T(1,128)S(1)} %pad_add_fusion.1.meta.places, f32[2,2,256,256]{3,2,1,0:T(8,128)} %probe_h.1, f32[2,264,256]{2,1,0:T(8,128)S(1)} %collective-permute-done.6.bottom, f32[2,264,256]{2,1,0:T(8,128)S(1)} %collective-permute-done.8.corner, f32[2,264,512]{2,1,0:T(8,128)S(1)} %collective-permute-done.7.lower), custom_call_target="tpu_custom_call" | custom-call | flops 4000000000 | bytes 4000000 | tf_op jit(solution)/shard_map/light/pallas_call | solution.py:177
  109.6 2.1 %collective-permute-done.9.other = f32[4,64,256]{2,1,0:T(8,128)S(1)} collective-permute-done((f32[4,64,256]{2,1,0:T(8,128)S(1)}, f32[4,64,256]{2,1,0:T(8,128)S(1)}, u32[]{:S(2)}, u32[]{:S(2)}) %collective-permute-start.9) | collective-permute-done | bytes 262176 | tf_op jit(solution)/shard_map/ppermute | solution.py:711
  111.7 0.6 join.2.mine
  112.3 0.2 collective-permute-start.10
  112.5 3.2 %finish_far.1.before = f32[2,512,512]{2,1,0:T(8,128)} custom-call(f32[2,512,512]{2,1,0:T(8,128)} %get-tuple-element.89.own, f32[2,264,256]{2,1,0:T(8,128)S(1)} %collective-permute-done.6.bottom, f32[2,264,512]{2,1,0:T(8,128)S(1)} %collective-permute-done.7.lower, f32[512,512]{1,0:T(8,128)S(1)} %light.1.scale, f32[2,512,512]{2,1,0:T(8,128)} %tile.13), custom_call_target="tpu_custom_call" | custom-call | flops 2000000000 | bytes 4000000 | tf_op jit(solution)/shard_map/finish_far/pallas_call | solution.py:640
  115.8 3.1 %collective-permute-done.11.top = f32[2,256,256]{2,1,0:T(8,128)S(1)} collective-permute-done((f32[2,256,256]{2,1,0:T(8,128)S(1)}, f32[2,256,256]{2,1,0:T(8,128)S(1)}, u32[]{:S(2)}, u32[]{:S(2)}) %collective-permute-start.11) | collective-permute-done | bytes 524320 | tf_op jit(solution)/shard_map/ppermute | solution.py:706
  118.9 1.9 %finish_near.1 = f32[2,512,512]{2,1,0:T(8,128)} custom-call(f32[2,512,512]{2,1,0:T(8,128)} %finish_far.1.before, f32[2,256,256]{2,1,0:T(8,128)S(1)} %collective-permute-done.11.top, f32[512,512]{1,0:T(8,128)S(1)} %light.1.scale), custom_call_target="tpu_custom_call", output_to_operand_aliasing={{}: (0, {})} | custom-call | flops 2000000000 | bytes 4000000 | tf_op jit(solution)/shard_map/finish_near/pallas_call | solution.py:684
  120.8 1.5 %join.3 = f32[4,256,256]{2,1,0:T(8,128)} custom-call(s32[1,24]{1,0:T(1,128)S(1)} %pad_add_fusion.1.meta.places, f32[4,128,256]{2,1,0:T(8,128)S(1)} %join.2.mine, f32[4,128,256]{2,1,0:T(8,128)S(1)} %collective-permute-done.10.other), custom_call_target="tpu_custom_call" | custom-call | bytes 2000000 | tf_op jit(solution)/shard_map/join/pallas_call | solution.py:900
  (24 shorter events, 0.8 us)
Async XLA Ops:
  2.8 6.0 %copy-start.1 = (s32[8,2]{0,1:T(2,128)S(1)}, s32[8,2]{0,1:T(2,128)}, u32[]{:S(2)}) copy-start(s32[8,2]{0,1:T(2,128)} %param.12) | copy-start | bytes 196
  2.8 17.8 %collective-permute-start = (f32[2,256,256]{2,1,0:T(8,128)}, f32[2,256,256]{2,1,0:T(8,128)S(1)}, u32[]{:S(2)}, u32[]{:S(2)}) collective-permute-start(f32[2,256,256]{2,1,0:T(8,128)} %get-tuple-element.52), channel_id=1, source_target_pairs={{1,0},{2,1},{3,2},{4,3},{5,4},{6,5},{7,6},{9,8},{10,9},{11,10},{12... | collective-permute-start | bytes 1572872 | tf_op jit(solution)/shard_map/ppermute | solution.py:706
  4.1 27.1 %collective-permute-start.2 = (f32[2,256,256]{2,1,0:T(8,128)}, f32[2,256,256]{2,1,0:T(8,128)S(1)}, u32[]{:S(2)}, u32[]{:S(2)}) collective-permute-start(f32[2,256,256]{2,1,0:T(8,128)} %get-tuple-element.57), channel_id=1, source_target_pairs={{1,0},{2,1},{3,2},{4,3},{5,4},{6,5},{7,6},{9,8},{10,9},{11,10},{12... | collective-permute-start | bytes 1572872 | tf_op jit(solution)/shard_map/ppermute | solution.py:706
  6.7 15.3 %collective-permute-start.1 = (f32[2,256,512]{2,1,0:T(8,128)S(1)}, f32[2,256,512]{2,1,0:T(8,128)S(1)}, u32[]{:S(2)}, u32[]{:S(2)}) collective-permute-start(f32[2,256,512]{2,1,0:T(8,128)S(1)} %cut_lower.1), channel_id=1, source_target_pairs={{8,0},{16,8},{24,16},{9,1},{17,9},{25,17},{10,2},{18,10},{26,18},{... | collective-permute-start | bytes 3145736 | tf_op jit(solution)/shard_map/ppermute | solution.py:706
  9.2 12.7 %copy-start = (f32[2,2,256,256]{3,2,1,0:T(8,128)S(1)}, f32[2,2,256,256]{3,2,1,0:T(8,128)}, u32[]{:S(2)}) copy-start(f32[2,2,256,256]{3,2,1,0:T(8,128)} %probe_h.1) | copy-start | bytes 3145732
  20.7 10.6 %collective-permute-start.3 = (f32[2,256,256]{2,1,0:T(8,128)S(1)}, f32[2,256,256]{2,1,0:T(8,128)S(1)}, u32[]{:S(2)}, u32[]{:S(2)}) collective-permute-start(f32[2,256,256]{2,1,0:T(8,128)S(1)} %collective-permute-done.refs_0_), channel_id=1, source_target_pairs={{8,0},{16,8},{24,16},{9,1},{17,9},{25,17},{10,2},{18,10},{26,18},{... | collective-permute-start | bytes 1572872 | tf_op jit(solution)/shard_map/ppermute | solution.py:706
  38.4 5.2 %collective-permute-start.4 = (f32[5,128,256]{2,1,0:T(8,128)S(1)}, f32[5,128,256]{2,1,0:T(8,128)S(1)}, u32[]{:S(2)}, u32[]{:S(2)}) collective-permute-start(f32[5,128,256]{2,1,0:T(8,128)S(1)} %get-tuple-element.71), channel_id=1, source_target_pairs={{0,8},{8,0},{16,24},{24,16},{1,9},{9,1},{17,25},{25,17},{2,10},{10... | collective-permute-start | bytes 1966088 | tf_op jit(solution)/shard_map/ppermute | solution.py:711
  41.9 13.6 %collective-permute-start.6 = (f32[2,264,256]{2,1,0:T(8,128)S(1)}, f32[2,264,256]{2,1,0:T(8,128)S(1)}, u32[]{:S(2)}, u32[]{:S(2)}) collective-permute-start(f32[2,264,256]{2,1,0:T(8,128)S(1)} %get-tuple-element.74), channel_id=1, source_target_pairs={{0,1},{1,2},{2,3},{3,4},{4,5},{5,6},{6,7},{8,9},{9,10},{10,11},{11... | collective-permute-start | bytes 1622024 | tf_op jit(solution)/shard_map/ppermute | solution.py:706
  44.2 15.2 %collective-permute-start.5 = (f32[5,64,256]{2,1,0:T(8,128)S(1)}, f32[5,64,256]{2,1,0:T(8,128)S(1)}, u32[]{:S(2)}, u32[]{:S(2)}) collective-permute-start(f32[5,64,256]{2,1,0:T(8,128)S(1)} %get-tuple-element.73), channel_id=1, source_target_pairs={{0,16},{8,24},{16,0},{24,8},{1,17},{9,25},{17,1},{25,9},{2,18},{10... | collective-permute-start | bytes 983048 | tf_op jit(solution)/shard_map/ppermute | solution.py:711
  59.4 25.1 %collective-permute-start.7 = (f32[2,264,512]{2,1,0:T(8,128)S(1)}, f32[2,264,512]{2,1,0:T(8,128)S(1)}, u32[]{:S(2)}, u32[]{:S(2)}) collective-permute-start(f32[2,264,512]{2,1,0:T(8,128)S(1)} %annotate.1), channel_id=1, source_target_pairs={{0,8},{8,16},{16,24},{1,9},{9,17},{17,25},{2,10},{10,18},{18,26},{... | collective-permute-start | bytes 3244040 | tf_op jit(solution)/shard_map/ppermute | solution.py:706
  84.5 18.2 %collective-permute-start.8 = (f32[2,264,256]{2,1,0:T(8,128)S(1)}, f32[2,264,256]{2,1,0:T(8,128)S(1)}, u32[]{:S(2)}, u32[]{:S(2)}) collective-permute-start(f32[2,264,256]{2,1,0:T(8,128)S(1)} %get-tuple-element.81), channel_id=1, source_target_pairs={{0,8},{8,16},{16,24},{1,9},{9,17},{17,25},{2,10},{10,18},{18,26},{... | collective-permute-start | bytes 1622024 | tf_op jit(solution)/shard_map/ppermute | solution.py:706
  102.8 8.9 %collective-permute-start.9 = (f32[4,64,256]{2,1,0:T(8,128)S(1)}, f32[4,64,256]{2,1,0:T(8,128)S(1)}, u32[]{:S(2)}, u32[]{:S(2)}) collective-permute-start(f32[4,64,256]{2,1,0:T(8,128)S(1)} %collect.1.mine), channel_id=1, source_target_pairs={{0,16},{8,24},{16,0},{24,8},{1,17},{9,25},{17,1},{25,9},{2,18},{10... | collective-permute-start | bytes 786440 | tf_op jit(solution)/shard_map/ppermute | solution.py:711
  104.7 14.2 %collective-permute-start.11 = (f32[2,256,256]{2,1,0:T(8,128)S(1)}, f32[2,256,256]{2,1,0:T(8,128)S(1)}, u32[]{:S(2)}, u32[]{:S(2)}) collective-permute-start(f32[2,256,256]{2,1,0:T(8,128)S(1)} %merge.1), channel_id=1, source_target_pairs={{0,1},{1,2},{2,3},{3,4},{4,5},{5,6},{6,7},{8,9},{9,10},{10,11},{11... | collective-permute-start | bytes 1572872 | tf_op jit(solution)/shard_map/ppermute | solution.py:706
  112.3 8.5 %collective-permute-start.10 = (f32[4,128,256]{2,1,0:T(8,128)S(1)}, f32[4,128,256]{2,1,0:T(8,128)S(1)}, u32[]{:S(2)}, u32[]{:S(2)}) collective-permute-start(f32[4,128,256]{2,1,0:T(8,128)S(1)} %join.2.mine), channel_id=1, source_target_pairs={{0,8},{8,0},{16,24},{24,16},{1,9},{9,1},{17,25},{25,17},{2,10},{10... | collective-permute-start | bytes 1572872 | tf_op jit(solution)/shard_map/ppermute | solution.py:711

commit v3 on v2

--- a/solution.py
+++ b/solution.py
@@ -367,17 +367,18 @@
                 for t, value in enumerate((parts[0][c] + parts[1][c], parts[0][c] - parts[1][c])):
                     x_f[t, 0, rows, cols], x_f[t, 1, rows, cols] = split(value)
 
-        def dft_rows(m, t):
-            cols = pl.ds(m * size, size)
-            high = x_f[t, 0, :, cols]
-            u = dot(three_left(forward_t, t), jnp.concatenate([high, x_f[t, 1, :, cols], high], axis=0))
-            rows = pl.ds(m * size + t * half, half)
-            for v, value in enumerate((u[:, :half] + u[:, half:], u[:, :half] - u[:, half:])):
-                high, low = split(value)
-                for c in range(2):
-                    lanes = pl.ds(c * half, half)
-                    y_f[v, 0, rows, lanes] = high[c * half : (c + 1) * half]
-                    y_f[v, 1, rows, lanes] = low[c * half : (c + 1) * half]
+        def dft_rows(t):
+            high = x_f[t, 0]
+            both = dot(three_left(forward_t, t), jnp.concatenate([high, x_f[t, 1], high], axis=0))
+            for m in range(modes):
+                left, right = both[:, m * size : m * size + half], both[:, m * size + half : (m + 1) * size]
+                rows = pl.ds(m * size + t * half, half)
+                for v, value in enumerate((left + right, left - right)):
+                    high, low = split(value)
+                    for c in range(2):
+                        lanes = pl.ds(c * half, half)
+                        y_f[v, 0, rows, lanes] = high[c * half : (c + 1) * half]
+                        y_f[v, 1, rows, lanes] = low[c * half : (c + 1) * half]
 
         def dft_cols(v):
             high = y_f[v, 0]
@@ -400,7 +401,7 @@
         pieces = [(take, at) for at in range(0, size, step)]
         for m in range(modes):
             pieces += [(fold_rows, m, at) for at in range(0, half, fine)]
-            pieces += [(dft_rows, m, t) for t in range(2)]
+        pieces += [(dft_rows, t) for t in range(2)]
         pieces += [(dft_cols, v) for v in range(2)]
         pieces += [(scale, v, at) for v in range(2) for at in range(0, size, fine)]
         return [functools.partial(*piece) for piece in pieces]
@@ -423,10 +424,11 @@
                     x_b[t, 0, spot, cols] = high[:, c * half : (c + 1) * half]
                     x_b[t, 1, spot, cols] = low[:, c * half : (c + 1) * half]
 
-        def dft_rows(m, t):
-            cols = pl.ds(m * size, size)
-            high = x_b[t, 0, :, cols]
-            back[m, t] = dot(three_left(backward_t, t), jnp.concatenate([high, x_b[t, 1, :, cols], high], axis=0))
+        def dft_rows(t):
+            high = x_b[t, 0]
+            both = dot(three_left(backward_t, t), jnp.concatenate([high, x_b[t, 1], high], axis=0))
+            for m in range(modes):
+                back[m, t] = both[:, m * size : (m + 1) * size]
 
         def gradients(at):
             waves = []
@@ -460,7 +462,7 @@
         pieces = [(dft_cols, v) for v in range(2)]
         for m in range(modes):
             pieces += [(unfold_cols, m, t, at) for t in range(2) for at in range(0, half, step)]
-            pieces += [(dft_rows, m, t) for t in range(2)]
+        pieces += [(dft_rows, t) for t in range(2)]
         pieces += [(gradients, at) for at in range(0, half, fine)]
         pieces += [(add, c) for c in range(2)]
         return [functools.partial(*piece) for piece in pieces]

time: 123 us -> 124 us (level)
  blocking collectives: 33.9 us -> 42.1 us
  starting transfers between devices: 29.3 us -> 23.2 us
  Pallas kernels: 35.6 us -> 32.1 us
  waiting for transfers between devices: 21.4 us -> 24.1 us
    ppermute x8, waiting for transfers between devices: 15.2 us -> 23.8 us  [from_behind(): return lax.ppermute(array, axis, pairs)]
    all_to_all x1, blocking collectives: 22 us -> 30.1 us  [body(): lax.all_to_all(deal([share, got], parts, rows), 'col', 0, 0, tiled=True)]
    ppermute x4, starting transfers between devices: 12.7 us -> 6.12 us  [exchange(): return lax.ppermute(array, axis, [(i, i ^ bit) for i in range(count)])]
    ppermute x4, waiting for transfers between devices: 6.19 us -> 0.25 us  [exchange(): return lax.ppermute(array, axis, [(i, i ^ bit) for i in range(count)])]
    pallas_call x1, Pallas kernels: 9.25 us -> 6.22 us  [visit_inside(): pl.pallas_call(kernel, out_shape=[field, field, pltpu.VMEM((2 * modes + 1...]
  transfers between devices with their start and end apart: 12 -> 12, of which waited for: 6 -> 5; matrix products, arithmetic and copies ran while one was open for 0% -> 0% of each run, Pallas kernels for 20% -> 17%
where the time goes in v3:
time: 124 us
  blocking collectives  42.1 us (34%)
  Pallas kernels  32.1 us (26%)
  waiting for transfers between devices  24.1 us (19%)
  starting transfers between devices  23.2 us (19%)
  between operations  1.69 us (1%)
    all_to_all x1, blocking collectives, body(): lax.all_to_all(deal([share, got], parts, rows), 'col', 0, 0, tiled=True)  30.1 us
    ppermute x8, waiting for transfers between devices, from_behind(): return lax.ppermute(array, axis, pairs)  23.8 us
    ppermute x8, starting transfers between devices, from_behind(): return lax.ppermute(array, axis, pairs)  17.1 us
    all_to_all x1, blocking collectives, body(): new = lax.all_to_all(new, 'col', 0, 0, tiled=True)  12 us
    pallas_call x1, Pallas kernels, visit_beyond(): pl.pallas_call(kernel, out_shape=[pltpu.VMEM(item.shape, item.dtype) for...  7.21 us
    pallas_call x1, Pallas kernels, visit_inside(): pl.pallas_call(kernel, out_shape=[field, field, pltpu.VMEM((2 * modes + 1...  6.22 us
    ppermute x4, starting transfers between devices, exchange(): return lax.ppermute(array, axis, [(i, i ^ bit) for i in range(count)])  6.12 us
    pallas_call x2, Pallas kernels, cut(): pl.pallas_call(kernel, out_shape=[jax.ShapeDtypeStruct((2, height, width)...  3.43 us
  transfers between devices with their start and end apart: 12, of which 5 were waited for; matrix products, arithmetic and copies ran while one was open for 0% of the time, Pallas kernels for 17%

profile of v3, /device:TPU:0, one launch (start us, length us, event | category | flops | bytes accessed | tf_op | source)
XLA Modules:
  0.0 123.8 jit_solution(10050891674128088937)
XLA Ops:
  0.6 2.2 %cut_right.1 = (f32[2,256,256]{2,1,0:T(8,128)}, f32[2,256,256]{2,1,0:T(8,128)}) custom-call(f32[2,512,512]{2,1,0:T(8,128)} %tile.13), custom_call_target="tpu_custom_call" | custom-call | bytes 1000000 | tf_op jit(solution)/shard_map/cut_right/pallas_call | solution.py:732
  2.8 1.3 %collective-permute-start = (f32[2,256,256]{2,1,0:T(8,128)}, f32[2,256,256]{2,1,0:T(8,128)S(1)}, u32[]{:S(2)}, u32[]{:S(2)}) collective-permute-start(f32[2,256,256]{2,1,0:T(8,128)} %get-tuple-element.52), channel_id=1, source_target_pairs={{1,0},{2,1},{3,2},{4,3},{5,4},{6,5},{7,6},{9,8},{10,9},{11,10},{12... | collective-permute-start | bytes 1572872 | tf_op jit(solution)/shard_map/ppermute | solution.py:708
  4.1 1.3 %collective-permute-start.2 = (f32[2,256,256]{2,1,0:T(8,128)}, f32[2,256,256]{2,1,0:T(8,128)S(1)}, u32[]{:S(2)}, u32[]{:S(2)}) collective-permute-start(f32[2,256,256]{2,1,0:T(8,128)} %get-tuple-element.57), channel_id=1, source_target_pairs={{1,0},{2,1},{3,2},{4,3},{5,4},{6,5},{7,6},{9,8},{10,9},{11,10},{12... | collective-permute-start | bytes 1572872 | tf_op jit(solution)/shard_map/ppermute | solution.py:708
  5.4 1.2 cut_lower.1
  6.7 1.3 %collective-permute-start.1 = (f32[2,256,512]{2,1,0:T(8,128)S(1)}, f32[2,256,512]{2,1,0:T(8,128)S(1)}, u32[]{:S(2)}, u32[]{:S(2)}) collective-permute-start(f32[2,256,512]{2,1,0:T(8,128)S(1)} %cut_lower.1), channel_id=1, source_target_pairs={{8,0},{16,8},{24,16},{9,1},{17,9},{25,17},{10,2},{18,10},{26,18},{... | collective-permute-start | bytes 3145736 | tf_op jit(solution)/shard_map/ppermute | solution.py:708
  8.7 0.1 broadcast_in_dim_tile.3
  9.1 0.1 stack.35
  9.2 3.0 %arrange.1.amplitudes = f32[8,256,256]{2,1,0:T(8,128)} custom-call(s32[1,24]{1,0:T(1,128)S(1)} %pad_add_fusion.1.meta.places, f32[8,256,256]{2,1,0:T(8,128)} %amplitudes.1), custom_call_target="tpu_custom_call" | custom-call | flops 30000001024 | bytes 4000000 | tf_op jit(solution)/shard_map/arrange/pallas_call | solution.py:244
  12.3 8.4 %collective-permute-done.refs_0_ = f32[2,256,256]{2,1,0:T(8,128)S(1)} collective-permute-done((f32[2,256,256]{2,1,0:T(8,128)}, f32[2,256,256]{2,1,0:T(8,128)S(1)}, u32[]{:S(2)}, u32[]{:S(2)}) %collective-permute-start) | collective-permute-done | bytes 524320 | tf_op jit(solution)/shard_map/ppermute | solution.py:708
  20.7 1.3 %collective-permute-start.3 = (f32[2,256,256]{2,1,0:T(8,128)S(1)}, f32[2,256,256]{2,1,0:T(8,128)S(1)}, u32[]{:S(2)}, u32[]{:S(2)}) collective-permute-start(f32[2,256,256]{2,1,0:T(8,128)S(1)} %collective-permute-done.refs_0_), channel_id=1, source_target_pairs={{8,0},{16,8},{24,16},{9,1},{17,9},{25,17},{10,2},{18,10},{26,18},{... | collective-permute-start | bytes 1572872 | tf_op jit(solution)/shard_map/ppermute | solution.py:708
  22.0 6.2 %slots_inside.1 = (f32[2,768,768]{2,1,0:T(8,128)S(1)}, f32[2,768,768]{2,1,0:T(8,128)S(1)}, f32[5,256,256]{2,1,0:T(8,128)S(1)}) custom-call(s32[1,24]{1,0:T(1,128)S(1)} %pad_add_fusion.1.meta.places, f32[2,2,256,256]{3,2,1,0:T(8,128)S(1)} %copy-done, f32[8,256,256]{2,1,0:T(8,128)} %arrange.1.amplitudes, f32[2,512,512]{2,1,0:T(8,128)} %tile.13, ...), custom_call_target="tpu_custom_call" | custom-call | flops 12000000000 | bytes 16000000 | tf_op jit(solution)/shard_map/slots_inside/pallas_call | solution.py:546
  28.2 2.9 %collective-permute-done.2.refs_1_ = f32[2,256,256]{2,1,0:T(8,128)S(1)} collective-permute-done((f32[2,256,256]{2,1,0:T(8,128)}, f32[2,256,256]{2,1,0:T(8,128)S(1)}, u32[]{:S(2)}, u32[]{:S(2)}) %collective-permute-start.2) | collective-permute-done | bytes 524320 | tf_op jit(solution)/shard_map/ppermute | solution.py:708
  31.1 7.2 %slots_beyond.1 = (f32[2,768,768]{2,1,0:T(8,128)S(1)}, f32[2,768,768]{2,1,0:T(8,128)S(1)}, f32[5,256,256]{2,1,0:T(8,128)S(1)}, f32[2,512,512]{2,1,0:T(8,128)}, f...) custom-call(s32[1,24]{1,0:T(1,128)S(1)} %pad_add_fusion.1.meta.place, ...), custom_call_target="tpu_custom_call", output_to_operand_aliasing={{0}: (9, {}), {1}: (10, {}), {2}: (11, {})} | custom-call | flops 12000000000 | bytes 16000000 | tf_op jit(solution)/shard_map/slots_beyond/pallas_call | solution.py:578
  38.3 5.2 %collective-permute-start.4 = (f32[5,128,256]{2,1,0:T(8,128)S(1)}, f32[5,128,256]{2,1,0:T(8,128)S(1)}, u32[]{:S(2)}, u32[]{:S(2)}) collective-permute-start(f32[5,128,256]{2,1,0:T(8,128)S(1)} %get-tuple-element.71), channel_id=1, source_target_pairs={{0,8},{8,0},{16,24},{24,16},{1,9},{9,1},{17,25},{25,17},{2,10},{10... | collective-permute-start | bytes 1966088 | tf_op jit(solution)/shard_map/ppermute | solution.py:713
  43.5 5.9 %collective-permute-start.6 = (f32[2,264,256]{2,1,0:T(8,128)S(1)}, f32[2,264,256]{2,1,0:T(8,128)S(1)}, u32[]{:S(2)}, u32[]{:S(2)}) collective-permute-start(f32[2,264,256]{2,1,0:T(8,128)S(1)} %get-tuple-element.74), channel_id=1, source_target_pairs={{0,1},{1,2},{2,3},{3,4},{4,5},{5,6},{6,7},{8,9},{9,10},{10,11},{11... | collective-permute-start | bytes 1622024 | tf_op jit(solution)/shard_map/ppermute | solution.py:708
  49.4 0.6 fold.1
  50.1 0.8 collective-permute-start.5
  50.8 10.5 %collective-permute-done.6.bottom = f32[2,264,256]{2,1,0:T(8,128)S(1)} collective-permute-done((f32[2,264,256]{2,1,0:T(8,128)S(1)}, f32[2,264,256]{2,1,0:T(8,128)S(1)}, u32[]{:S(2)}, u32[]{:S(2)}) %collective-permute-start.6) | collective-permute-done | bytes 540704 | tf_op jit(solution)/shard_map/ppermute | solution.py:708
  61.3 1.4 %collective-permute-start.7 = (f32[2,264,512]{2,1,0:T(8,128)S(1)}, f32[2,264,512]{2,1,0:T(8,128)S(1)}, u32[]{:S(2)}, u32[]{:S(2)}) collective-permute-start(f32[2,264,512]{2,1,0:T(8,128)S(1)} %annotate.1), channel_id=1, source_target_pairs={{0,8},{8,16},{16,24},{1,9},{9,17},{17,25},{2,10},{10,18},{18,26},{... | collective-permute-start | bytes 3244040 | tf_op jit(solution)/shard_map/ppermute | solution.py:708
  62.8 30.1 %all_to_all.10.pieces = f32[8,5,8,256]{3,2,1,0:T(8,128)S(1)} all-to-all(f32[8,5,8,256]{3,2,1,0:T(8,128)S(1)} %deal.1), channel_id=1, replica_groups=mesh['row'=4,'col'=8] {'col'}, dimensions={0} | all-to-all | bytes 655360 | tf_op jit(solution)/shard_map/all_to_all | solution.py:966
  92.8 1.3 %settle.1 = f32[8,4,8,256]{3,2,1,0:T(8,128)S(1)} custom-call(s32[1,24]{1,0:T(1,128)S(1)} %pad_add_fusion.1.meta.places, f32[4,256,256]{2,1,0:T(8,128)} %bitcast.13, f32[8,5,8,256]{3,2,1,0:T(8,128)S(1)} %all_to_all.10.pieces), custom_call_target="tpu_custom_call" | custom-call | bytes 1000000 | tf_op jit(solution)/shard_map/settle/pallas_call | solution.py:854
  94.2 1.3 %collective-permute-start.8 = (f32[2,264,256]{2,1,0:T(8,128)S(1)}, f32[2,264,256]{2,1,0:T(8,128)S(1)}, u32[]{:S(2)}, u32[]{:S(2)}) collective-permute-start(f32[2,264,256]{2,1,0:T(8,128)S(1)} %get-tuple-element.81), channel_id=1, source_target_pairs={{0,8},{8,16},{16,24},{1,9},{9,17},{17,25},{2,10},{10,18},{18,26},{... | collective-permute-start | bytes 1622024 | tf_op jit(solution)/shard_map/ppermute | solution.py:708
  95.5 12.0 %all_to_all.11.pieces = f32[8,4,8,256]{3,2,1,0:T(8,128)S(1)} all-to-all(f32[8,4,8,256]{3,2,1,0:T(8,128)S(1)} %settle.1), channel_id=1, replica_groups=mesh['row'=4,'col'=8] {'col'}, dimensions={0} | all-to-all | bytes 524288 | tf_op jit(solution)/shard_map/all_to_all | solution.py:973
  107.6 0.1 merge.1
  107.8 3.4 %collective-permute-start.11 = (f32[2,256,256]{2,1,0:T(8,128)S(1)}, f32[2,256,256]{2,1,0:T(8,128)S(1)}, u32[]{:S(2)}, u32[]{:S(2)}) collective-permute-start(f32[2,256,256]{2,1,0:T(8,128)S(1)} %merge.1), channel_id=1, source_target_pairs={{0,1},{1,2},{2,3},{3,4},{4,5},{5,6},{6,7},{8,9},{9,10},{10,11},{11... | collective-permute-start | bytes 1572872 | tf_op jit(solution)/shard_map/ppermute | solution.py:708
  111.1 2.7 %light.1.scale = f32[512,512]{1,0:T(8,128)S(1)} custom-call(s32[1,24]{1,0:T(1,128)S(1)} %pad_add_fusion.1.meta.places, f32[2,2,256,256]{3,2,1,0:T(8,128)} %probe_h.1, f32[2,264,256]{2,1,0:T(8,128)S(1)} %collective-permute-done.6.bottom, f32[2,264,256]{2,1,0:T(8,128)S(1)} %collective-permute-done.8.corner, f32[2,264,512]{2,1,0:T(8,128)S(1)} %collective-permute-done.7.lower), custom_call_target="tpu_custom_call" | custom-call | flops 4000000000 | bytes 4000000 | tf_op jit(solution)/shard_map/light/pallas_call | solution.py:177
  113.9 0.2 collective-permute-done.9.other
  114.1 0.6 join.2.mine
  114.8 3.2 %finish_far.1.before = f32[2,512,512]{2,1,0:T(8,128)} custom-call(f32[2,512,512]{2,1,0:T(8,128)} %get-tuple-element.89.own, f32[2,264,256]{2,1,0:T(8,128)S(1)} %collective-permute-done.6.bottom, f32[2,264,512]{2,1,0:T(8,128)S(1)} %collective-permute-done.7.lower, f32[512,512]{1,0:T(8,128)S(1)} %light.1.scale, f32[2,512,512]{2,1,0:T(8,128)} %tile.13), custom_call_target="tpu_custom_call" | custom-call | flops 2000000000 | bytes 4000000 | tf_op jit(solution)/shard_map/finish_far/pallas_call | solution.py:642
  118.0 2.1 %collective-permute-done.11.top = f32[2,256,256]{2,1,0:T(8,128)S(1)} collective-permute-done((f32[2,256,256]{2,1,0:T(8,128)S(1)}, f32[2,256,256]{2,1,0:T(8,128)S(1)}, u32[]{:S(2)}, u32[]{:S(2)}) %collective-permute-start.11) | collective-permute-done | bytes 524320 | tf_op jit(solution)/shard_map/ppermute | solution.py:708
  120.1 1.9 %finish_near.1 = f32[2,512,512]{2,1,0:T(8,128)} custom-call(f32[2,512,512]{2,1,0:T(8,128)} %finish_far.1.before, f32[2,256,256]{2,1,0:T(8,128)S(1)} %collective-permute-done.11.top, f32[512,512]{1,0:T(8,128)S(1)} %light.1.scale), custom_call_target="tpu_custom_call", output_to_operand_aliasing={{}: (0, {})} | custom-call | flops 2000000000 | bytes 4000000 | tf_op jit(solution)/shard_map/finish_near/pallas_call | solution.py:686
  122.1 1.5 %join.3 = f32[4,256,256]{2,1,0:T(8,128)} custom-call(s32[1,24]{1,0:T(1,128)S(1)} %pad_add_fusion.1.meta.places, f32[4,128,256]{2,1,0:T(8,128)S(1)} %join.2.mine, f32[4,128,256]{2,1,0:T(8,128)S(1)} %collective-permute-done.10.other), custom_call_target="tpu_custom_call" | custom-call | bytes 2000000 | tf_op jit(solution)/shard_map/join/pallas_call | solution.py:902
  (24 shorter events, 0.7 us)
Async XLA Ops:
  2.8 6.0 %copy-start.1 = (s32[8,2]{0,1:T(2,128)S(1)}, s32[8,2]{0,1:T(2,128)}, u32[]{:S(2)}) copy-start(s32[8,2]{0,1:T(2,128)} %param.12) | copy-start | bytes 196
  2.8 17.8 %collective-permute-start = (f32[2,256,256]{2,1,0:T(8,128)}, f32[2,256,256]{2,1,0:T(8,128)S(1)}, u32[]{:S(2)}, u32[]{:S(2)}) collective-permute-start(f32[2,256,256]{2,1,0:T(8,128)} %get-tuple-element.52), channel_id=1, source_target_pairs={{1,0},{2,1},{3,2},{4,3},{5,4},{6,5},{7,6},{9,8},{10,9},{11,10},{12... | collective-permute-start | bytes 1572872 | tf_op jit(solution)/shard_map/ppermute | solution.py:708
  4.1 26.9 %collective-permute-start.2 = (f32[2,256,256]{2,1,0:T(8,128)}, f32[2,256,256]{2,1,0:T(8,128)S(1)}, u32[]{:S(2)}, u32[]{:S(2)}) collective-permute-start(f32[2,256,256]{2,1,0:T(8,128)} %get-tuple-element.57), channel_id=1, source_target_pairs={{1,0},{2,1},{3,2},{4,3},{5,4},{6,5},{7,6},{9,8},{10,9},{11,10},{12... | collective-permute-start | bytes 1572872 | tf_op jit(solution)/shard_map/ppermute | solution.py:708
  6.7 15.3 %collective-permute-start.1 = (f32[2,256,512]{2,1,0:T(8,128)S(1)}, f32[2,256,512]{2,1,0:T(8,128)S(1)}, u32[]{:S(2)}, u32[]{:S(2)}) collective-permute-start(f32[2,256,512]{2,1,0:T(8,128)S(1)} %cut_lower.1), channel_id=1, source_target_pairs={{8,0},{16,8},{24,16},{9,1},{17,9},{25,17},{10,2},{18,10},{26,18},{... | collective-permute-start | bytes 3145736 | tf_op jit(solution)/shard_map/ppermute | solution.py:708
  9.2 12.7 %copy-start = (f32[2,2,256,256]{3,2,1,0:T(8,128)S(1)}, f32[2,2,256,256]{3,2,1,0:T(8,128)}, u32[]{:S(2)}) copy-start(f32[2,2,256,256]{3,2,1,0:T(8,128)} %probe_h.1) | copy-start | bytes 3145732
  20.7 10.4 %collective-permute-start.3 = (f32[2,256,256]{2,1,0:T(8,128)S(1)}, f32[2,256,256]{2,1,0:T(8,128)S(1)}, u32[]{:S(2)}, u32[]{:S(2)}) collective-permute-start(f32[2,256,256]{2,1,0:T(8,128)S(1)} %collective-permute-done.refs_0_), channel_id=1, source_target_pairs={{8,0},{16,8},{24,16},{9,1},{17,9},{25,17},{10,2},{18,10},{26,18},{... | collective-permute-start | bytes 1572872 | tf_op jit(solution)/shard_map/ppermute | solution.py:708
  38.3 11.1 %collective-permute-start.4 = (f32[5,128,256]{2,1,0:T(8,128)S(1)}, f32[5,128,256]{2,1,0:T(8,128)S(1)}, u32[]{:S(2)}, u32[]{:S(2)}) collective-permute-start(f32[5,128,256]{2,1,0:T(8,128)S(1)} %get-tuple-element.71), channel_id=1, source_target_pairs={{0,8},{8,0},{16,24},{24,16},{1,9},{9,1},{17,25},{25,17},{2,10},{10... | collective-permute-start | bytes 1966088 | tf_op jit(solution)/shard_map/ppermute | solution.py:713
  43.5 17.8 %collective-permute-start.6 = (f32[2,264,256]{2,1,0:T(8,128)S(1)}, f32[2,264,256]{2,1,0:T(8,128)S(1)}, u32[]{:S(2)}, u32[]{:S(2)}) collective-permute-start(f32[2,264,256]{2,1,0:T(8,128)S(1)} %get-tuple-element.74), channel_id=1, source_target_pairs={{0,1},{1,2},{2,3},{3,4},{4,5},{5,6},{6,7},{8,9},{9,10},{10,11},{11... | collective-permute-start | bytes 1622024 | tf_op jit(solution)/shard_map/ppermute | solution.py:708
  50.1 11.2 %collective-permute-start.5 = (f32[5,64,256]{2,1,0:T(8,128)S(1)}, f32[5,64,256]{2,1,0:T(8,128)S(1)}, u32[]{:S(2)}, u32[]{:S(2)}) collective-permute-start(f32[5,64,256]{2,1,0:T(8,128)S(1)} %get-tuple-element.73), channel_id=1, source_target_pairs={{0,16},{8,24},{16,0},{24,8},{1,17},{9,25},{17,1},{25,9},{2,18},{10... | collective-permute-start | bytes 983048 | tf_op jit(solution)/shard_map/ppermute | solution.py:713
  61.3 32.9 %collective-permute-start.7 = (f32[2,264,512]{2,1,0:T(8,128)S(1)}, f32[2,264,512]{2,1,0:T(8,128)S(1)}, u32[]{:S(2)}, u32[]{:S(2)}) collective-permute-start(f32[2,264,512]{2,1,0:T(8,128)S(1)} %annotate.1), channel_id=1, source_target_pairs={{0,8},{8,16},{16,24},{1,9},{9,17},{17,25},{2,10},{10,18},{18,26},{... | collective-permute-start | bytes 3244040 | tf_op jit(solution)/shard_map/ppermute | solution.py:708
  94.2 13.4 %collective-permute-start.8 = (f32[2,264,256]{2,1,0:T(8,128)S(1)}, f32[2,264,256]{2,1,0:T(8,128)S(1)}, u32[]{:S(2)}, u32[]{:S(2)}) collective-permute-start(f32[2,264,256]{2,1,0:T(8,128)S(1)} %get-tuple-element.81), channel_id=1, source_target_pairs={{0,8},{8,16},{16,24},{1,9},{9,17},{17,25},{2,10},{10,18},{18,26},{... | collective-permute-start | bytes 1622024 | tf_op jit(solution)/shard_map/ppermute | solution.py:708
  107.7 6.4 %collective-permute-start.9 = (f32[4,64,256]{2,1,0:T(8,128)S(1)}, f32[4,64,256]{2,1,0:T(8,128)S(1)}, u32[]{:S(2)}, u32[]{:S(2)}) collective-permute-start(f32[4,64,256]{2,1,0:T(8,128)S(1)} %collect.1.mine), channel_id=1, source_target_pairs={{0,16},{8,24},{16,0},{24,8},{1,17},{9,25},{17,1},{25,9},{2,18},{10... | collective-permute-start | bytes 786440 | tf_op jit(solution)/shard_map/ppermute | solution.py:713
  107.8 12.4 %collective-permute-start.11 = (f32[2,256,256]{2,1,0:T(8,128)S(1)}, f32[2,256,256]{2,1,0:T(8,128)S(1)}, u32[]{:S(2)}, u32[]{:S(2)}) collective-permute-start(f32[2,256,256]{2,1,0:T(8,128)S(1)} %merge.1), channel_id=1, source_target_pairs={{0,1},{1,2},{2,3},{3,4},{4,5},{5,6},{6,7},{8,9},{9,10},{10,11},{11... | collective-permute-start | bytes 1572872 | tf_op jit(solution)/shard_map/ppermute | solution.py:708
  114.7 7.3 %collective-permute-start.10 = (f32[4,128,256]{2,1,0:T(8,128)S(1)}, f32[4,128,256]{2,1,0:T(8,128)S(1)}, u32[]{:S(2)}, u32[]{:S(2)}) collective-permute-start(f32[4,128,256]{2,1,0:T(8,128)S(1)} %join.2.mine), channel_id=1, source_target_pairs={{0,8},{8,0},{16,24},{24,16},{1,9},{9,1},{17,25},{25,17},{2,10},{10... | collective-permute-start | bytes 1572872 | tf_op jit(solution)/shard_map/ppermute | solution.py:713
